TPU v7x, 512 devices: a whole 4x8x8 slice. The times are simulated.
512 devices in a mesh: expert: 64 (over x, y, core), hsplit: 8 (over z).
Axes of the slice: x: 4, y: 8, z: 8, core: 2. Of those that a mesh axis runs over, the one named last changes fastest.
Arguments:
- tokens: bfloat16 [1024, 7168], P('expert'), may hold values from -6 to 6
- routes: int32 [1024, 8], P('expert'), may hold values from 0 to 15, all different within a row; in each aligned block of 4 rows (0 to 3, 4 to 7, ...) at most 4 rows name the same one
- route_weights: float32 [1024, 8], P('expert'), may hold values from 0.05 to 0.6
- gate_weight: bfloat16 [64, 1792, 2048], P('expert', None, 'hsplit'), may hold values from -0.0625 to 0.0625
- up_weight: bfloat16 [64, 1792, 2048], P('expert', None, 'hsplit'), may hold values from -0.0625 to 0.0625
- down_weight: bfloat16 [64, 2048, 1792], P('expert', 'hsplit'), may hold values from -0.125 to 0.125
Outputs:
- routed_out: bfloat16 [1024, 7168], P('expert', 'hsplit')
Inputs may be any that keep to these rules, and one draw needn't show every extreme that they name: `routes`: each token names 8 different experts. In each aligned block of 4 tokens (one of 4 blocks of the tokens of one index of the expert axis) some expert is named by every token of the block.
All inputs are finite; a program needn't handle non-finite values.
Results may differ from a plain program's by a relative error of at most 0.02.
Values may be sent and summed in bfloat16 or wider, within the bound.
A program may use at most 128 MiB of HBM per device.

v0:
```python
import jax
import jax.numpy as jnp
from jax import lax
from jax.sharding import PartitionSpec as P

EXPERTS = 16


def as_sent(array):

    def short(part):
        return part.astype(jnp.bfloat16) if part.dtype == jnp.float32 else part

    return jax.tree.map(short, array)


def swapped(block, axis, apart):
    count = lax.axis_size(axis)
    route = []
    for low in range(count):
        high = low | 1 << apart
        if high != low and high < count:
            route += [(low, high), (high, low)]
    return lax.ppermute(block, axis, route)


def expert_rows(tok_rows, full_gate, full_up, full_down):
    gate_value = jnp.dot(tok_rows, full_gate, preferred_element_type=jnp.float32)
    up_value = jnp.dot(tok_rows, full_up, preferred_element_type=jnp.float32)
    hidden = (jax.nn.silu(gate_value) * up_value).astype(jnp.bfloat16)
    partial_value = jnp.dot(hidden, full_down, preferred_element_type=jnp.float32)
    return lax.optimization_barrier(partial_value.astype(jnp.bfloat16))


def local(tokens, routes, route_weights, gate_weight, up_weight, down_weight):
    tok_dev, model_width = tokens.shape
    top_k = routes.shape[1]
    owners = lax.axis_size("expert")
    splits = lax.axis_size("hsplit")
    group_size = owners // EXPERTS
    group_bits = group_size.bit_length() - 1
    most = tok_dev // group_size
    slot_count = owners * most
    slice_width = model_width // group_size
    piece_width = slice_width // splits
    position = lax.axis_index("expert")
    token_group = lax.broadcasted_iota(jnp.int32, (tok_dev, top_k), 0) // most
    owner_of = (group_size * routes + token_group).reshape(-1)
    owner_hit = (owner_of[:, None] == jnp.arange(owners, dtype=jnp.int32)[None, :]).astype(
        jnp.int32
    )
    earlier = jnp.cumsum(owner_hit, axis=0) - owner_hit
    ranking = jnp.sum(earlier * owner_hit, axis=1)
    slot_of = owner_of * most + ranking
    slot_grid = slot_of.reshape(tok_dev, top_k)
    selector = jnp.any(
        slot_grid[:, :, None] == jnp.arange(slot_count, dtype=jnp.int32)[None, None, :], axis=1
    ).astype(jnp.bfloat16)
    outgoing = jnp.einsum("ts,td->sd", selector, tokens, preferred_element_type=jnp.float32).astype(
        jnp.bfloat16
    )
    outgoing = outgoing.reshape(owners, most, model_width)
    stacked = (gate_weight, up_weight, down_weight)
    for level in range(group_bits):
        partner = jax.tree.map(
            lambda part, own: part.astype(own.dtype),
            swapped(as_sent(stacked), "expert", level),
            stacked,
        )
        upper = position >> level & 1 == 1
        stacked = tuple(
            (
                jnp.where(
                    upper,
                    jnp.concatenate([far_piece, near_piece], axis=0),
                    jnp.concatenate([near_piece, far_piece], axis=0),
                )
                for near_piece, far_piece in zip(stacked, partner)
            )
        )
    share_units = gate_weight.shape[2]
    full_gate = stacked[0].reshape(model_width, share_units)
    full_up = stacked[1].reshape(model_width, share_units)
    full_down = stacked[2].transpose(1, 0, 2).reshape(share_units, group_size, splits, piece_width)
    full_down = full_down.transpose(0, 2, 1, 3).reshape(share_units, model_width)
    arrived = lax.all_to_all(outgoing, "expert", split_axis=0, concat_axis=0, tiled=True)
    flat_rows = arrived.reshape(-1, model_width)
    partials = expert_rows(flat_rows, full_gate, full_up, full_down).reshape(arrived.shape)
    partials = partials.reshape(slot_count, model_width)
    summed = lax.psum_scatter(
        partials.astype(jnp.float32).astype(jnp.bfloat16), "hsplit", scatter_dimension=1, tiled=True
    )
    results = summed.reshape(owners, most, -1)
    returned = lax.all_to_all(results, "expert", split_axis=0, concat_axis=0, tiled=True)
    picked = returned.reshape(slot_count, -1)[slot_of].astype(jnp.float32)
    weighted = picked.reshape(tok_dev, top_k, -1) * route_weights[:, :, None]
    return jnp.sum(weighted, axis=1).astype(jnp.bfloat16)


def solution(mesh):
    placed = (
        P("expert", None),
        P("expert", None),
        P("expert", None),
        P("expert", None, "hsplit"),
        P("expert", None, "hsplit"),
        P("expert", "hsplit", None),
    )
    return jax.shard_map(
        local, mesh=mesh, in_specs=placed, out_specs=P("expert", "hsplit"), check_vma=False
    )
```

profile of v0, /device:TPU:1, one launch (start us, length us, event | category | flops | bytes accessed | tf_op | source)
XLA Modules:
  0.0 355.0 jit_solution(12375925999608812411)
XLA Ops:
  8.2 2.9 convolution_convert_fusion.1
  11.1 7.0 %reshape.85 = bf16[64,4,7168]{2,1,0:T(4,128)(2,1)} reshape(bf16[256,7168]{1,0:T(8,128)(2,1)} %convolution_convert_fusion.1) | data formatting | bytes 7340032 | tf_op jit(solution)/shard_map/reshape | solution.py:62
  18.2 12.0 %all-to-all-start = ((bf16[64,4,7168]{2,1,0:T(4,128)(2,1)}), bf16[64,4,7168]{2,1,0:T(4,128)(2,1)}, u32[]{:S(2)}, u32[]{:S(2)}) async-start(bf16[64,4,7168]{2,1,0:T(4,128)(2,1)} %reshape.85), calls=%async_computation | async-start | bytes 7340032 | tf_op jit(solution)/shard_map/all_to_all | solution.py:86
  30.7 2.5 collective-permute-start.4
  35.2 2.4 collective-permute-start.2
  39.4 3.0 collective-permute-start.5
  42.5 3.6 %maximum_select_fusion.3 = bf16[2,1792,256]{2,1,0:T(8,128)(2,1)} fusion(bf16[1,1792,256]{2,1,0:T(8,128)(2,1)} %param.9, bf16[1,1792,256]{2,1,0:T(8,128)(2,1)} %collective-permute-done, pred[]{:T(512)S(6)} %eq.42), kind=kLoop, calls=%fused_computation.6 | loop fusion | flops 2752512 | bytes 3670017 | tf_op jit(solution)/shard_map/jit(_where)/select_n | solution.py:73
  46.0 2.2 collective-permute-start.1
  48.3 3.6 %maximum_select_fusion.4 = bf16[2,1792,256]{2,1,0:T(8,128)(2,1)} fusion(bf16[1,1792,256]{2,1,0:T(8,128)(2,1)} %param.10, bf16[1,1792,256]{2,1,0:T(8,128)(2,1)} %collective-permute-done.2, pred[]{:T(512)S(6)} %eq.42), kind=kLoop, calls=%fused_computation.7 | loop fusion | flops 2752512 | bytes 3670017 | tf_op jit(solution)/shard_map/jit(_where)/select_n | solution.py:73
  51.8 3.0 collective-permute-start.3
  54.9 95.2 %collective-permute-done.5 = bf16[2,256,1792]{1,2,0:T(8,128)(2,1)} collective-permute-done((bf16[2,256,1792]{1,2,0:T(8,128)(2,1)S(1)}, bf16[2,256,1792]{1,2,0:T(8,128)(2,1)}, u32[]{:S(2)}, u32[]{:S(2)}) %collective-permute-start.5) | collective-permute-done | bytes 1835040 | tf_op jit(solution)/shard_map/ppermute | solution.py:24
  150.1 2.4 maximum_select_fusion.2
  152.5 2.2 copy.25
  154.7 34.7 %collective-permute-done.1 = bf16[2,1792,256]{2,1,0:T(8,128)(2,1)} collective-permute-done((bf16[2,1792,256]{2,1,0:T(8,128)(2,1)}, bf16[2,1792,256]{2,1,0:T(8,128)(2,1)}, u32[]{:S(2)}, u32[]{:S(2)}) %collective-permute-start.1) | collective-permute-done | bytes 1835040 | tf_op jit(solution)/shard_map/ppermute | solution.py:24
  189.4 4.7 %maximum_select_fusion = bf16[4,1792,256]{2,1,0:T(8,128)(2,1)} fusion(bf16[2,1792,256]{2,1,0:T(8,128)(2,1)} %maximum_select_fusion.3, bf16[2,1792,256]{2,1,0:T(8,128)(2,1)} %collective-permute-done.1, pred[]{:T(512)S(6)} %eq.41), kind=kLoop, calls=%fused_computation.3 | loop fusion | flops 5505024 | bytes 7340033 | tf_op jit(solution)/shard_map/jit(_where)/select_n | solution.py:73
  194.0 34.7 %collective-permute-done.3 = bf16[2,1792,256]{2,1,0:T(8,128)(2,1)} collective-permute-done((bf16[2,1792,256]{2,1,0:T(8,128)(2,1)}, bf16[2,1792,256]{2,1,0:T(8,128)(2,1)}, u32[]{:S(2)}, u32[]{:S(2)}) %collective-permute-start.3) | collective-permute-done | bytes 1835040 | tf_op jit(solution)/shard_map/ppermute | solution.py:24
  228.7 4.8 %maximum_select_fusion.1 = bf16[4,1792,256]{2,1,0:T(8,128)(2,1)} fusion(bf16[2,1792,256]{2,1,0:T(8,128)(2,1)} %maximum_select_fusion.4, bf16[2,1792,256]{2,1,0:T(8,128)(2,1)} %collective-permute-done.3, pred[]{:T(512)S(6)} %eq.41), kind=kLoop, calls=%fused_computation.4 | loop fusion | flops 5505024 | bytes 7340033 | tf_op jit(solution)/shard_map/jit(_where)/select_n | solution.py:73
  233.5 6.8 %reshape.86 = bf16[256,7168]{1,0:T(8,128)(2,1)} reshape(bf16[64,4,7168]{2,1,0:T(4,128)(2,1)} %all-to-all-done) | data formatting | bytes 7340032 | tf_op jit(solution)/shard_map/reshape | solution.py:87
  240.2 4.3 %fusion.9 = f32[256,256]{1,0:T(8,128)S(1)} fusion(bf16[256,7168]{1,0:T(8,128)(2,1)} %reshape.86, bf16[7168,256]{1,0:T(8,128)(2,1)} %bitcast.30), kind=kOutput, calls=%fused_computation.32 | convolution fusion | flops 939524096 | bytes 7602176 | tf_op jit(solution)/shard_map/dot_general | solution.py:28
  244.5 10.0 %convolution_convert_fusion = bf16[256,7168]{1,0:T(8,128)(2,1)} fusion(bf16[256,7168]{0,1:T(8,128)(2,1)} %bitcast.26, f32[256,256]{1,0:T(8,128)S(1)} %fusion.9, bf16[256,7168]{1,0:T(8,128)(2,1)} %reshape.86, bf16[7168,256]{1,0:T(8,128)(2,1)} %bitcast.27), kind=kOutput, calls=%fused_computation.1 | convolution fusion | flops 1881276416 | bytes 14942208 | tf_op jit(solution)/shard_map/dot_general | solution.py:31
  254.5 5.9 %copy.27 = bf16[256,7168]{0,1:T(8,128)(2,1)} copy(bf16[256,7168]{1,0:T(8,128)(2,1)} %convolution_convert_fusion) | data formatting | bytes 7340032
  260.4 57.5 %reduce-scatter.4.cloned.1.call-done = bf16[896,256]{1,0:T(8,128)(2,1)} async-done(((bf16[7168,256]{1,0:T(8,128)(2,1)}), bf16[896,256]{1,0:T(8,128)(2,1)}) %reduce-scatter.4.cloned.1.call-update) | async-done | bytes 458768
  320.1 10.3 %all-to-all-start.1 = ((bf16[64,4,896]{2,1,0:T(4,128)(2,1)}), bf16[64,4,896]{2,1,0:T(4,128)(2,1)S(1)}, u32[]{:S(2)}, u32[]{:S(2)}) async-start(bf16[64,4,896]{2,1,0:T(4,128)(2,1)} %reshape.89), calls=%async_computation.1 | async-start | bytes 917504 | tf_op jit(solution)/shard_map/all_to_all | solution.py:94
  330.6 15.7 %all-to-all-done.1 = bf16[64,4,896]{2,1,0:T(4,128)(2,1)S(1)} async-done(((bf16[64,4,896]{2,1,0:T(4,128)(2,1)}), bf16[64,4,896]{2,1,0:T(4,128)(2,1)S(1)}, u32[]{:S(2)}, u32[]{:S(2)}) %all-to-all-start.1) | async-done | bytes 458784 | tf_op jit(solution)/shard_map/all_to_all | solution.py:94
  (35 shorter events, 10.0 us)
Async XLA Ops:
  6.5 1.7 copy-start
  18.2 12.0 %copy-start.1 = (bf16[1,256,1792]{2,1,0:T(8,128)(2,1)S(1)}, bf16[1,256,1792]{2,1,0:T(8,128)(2,1)}, u32[]{:S(2)}) copy-start(bf16[1,256,1792]{2,1,0:T(8,128)(2,1)} %param.11) | copy-start | bytes 2752516
  18.2 215.3 %all-to-all-start = ((bf16[64,4,7168]{2,1,0:T(4,128)(2,1)}), bf16[64,4,7168]{2,1,0:T(4,128)(2,1)}, u32[]{:S(2)}, u32[]{:S(2)}) async-start(bf16[64,4,7168]{2,1,0:T(4,128)(2,1)} %reshape.85), calls=%async_computation | async-start | bytes 7340032 | tf_op jit(solution)/shard_map/all_to_all | solution.py:86
  30.1 287.8 %reduce-scatter.4.cloned.1.call-start = ((), (), s32[]{:S(2)}) async-start(), calls=%async_computation.3 | async-start | bytes 4128768
  30.7 6.9 %collective-permute-start.4 = (bf16[1,256,1792]{1,2,0:T(8,128)(2,1)S(1)}, bf16[1,256,1792]{1,2,0:T(8,128)(2,1)}, u32[]{:S(2)}, u32[]{:S(2)}) collective-permute-start(bf16[1,256,1792]{1,2,0:T(8,128)(2,1)S(1)} %copy.22), channel_id=1, source_target_pairs={{0,8},{8,0},{16,24},{24,16},{32,40},{40,32},{48,56},{56,48},{64,72... | collective-permute-start | bytes 2752520 | tf_op jit(solution)/shard_map/ppermute | solution.py:24
  33.3 9.1 %collective-permute-start = (bf16[1,1792,256]{2,1,0:T(8,128)(2,1)}, bf16[1,1792,256]{2,1,0:T(8,128)(2,1)}, u32[]{:S(2)}, u32[]{:S(2)}) collective-permute-start(bf16[1,1792,256]{2,1,0:T(8,128)(2,1)} %param.9), channel_id=1, source_target_pairs={{0,8},{8,0},{16,24},{24,16},{32,40},{40,32},{48,56},{56,48},{64,72... | collective-permute-start | bytes 2752520 | tf_op jit(solution)/shard_map/ppermute | solution.py:24
  35.2 13.0 %collective-permute-start.2 = (bf16[1,1792,256]{2,1,0:T(8,128)(2,1)}, bf16[1,1792,256]{2,1,0:T(8,128)(2,1)}, u32[]{:S(2)}, u32[]{:S(2)}) collective-permute-start(bf16[1,1792,256]{2,1,0:T(8,128)(2,1)} %param.10), channel_id=1, source_target_pairs={{0,8},{8,0},{16,24},{24,16},{32,40},{40,32},{48,56},{56,48},{64,72... | collective-permute-start | bytes 2752520 | tf_op jit(solution)/shard_map/ppermute | solution.py:24
  39.4 110.7 %collective-permute-start.5 = (bf16[2,256,1792]{1,2,0:T(8,128)(2,1)S(1)}, bf16[2,256,1792]{1,2,0:T(8,128)(2,1)}, u32[]{:S(2)}, u32[]{:S(2)}) collective-permute-start(bf16[2,256,1792]{1,2,0:T(8,128)(2,1)S(1)} %maximum_select_fusion.5), channel_id=1, source_target_pairs={{0,16},{16,0},{8,24},{24,8},{32,48},{48,32},{40,56},{56,40},{64,80... | collective-permute-start | bytes 5505032 | tf_op jit(solution)/shard_map/ppermute | solution.py:24
  46.0 143.4 %collective-permute-start.1 = (bf16[2,1792,256]{2,1,0:T(8,128)(2,1)}, bf16[2,1792,256]{2,1,0:T(8,128)(2,1)}, u32[]{:S(2)}, u32[]{:S(2)}) collective-permute-start(bf16[2,1792,256]{2,1,0:T(8,128)(2,1)} %maximum_select_fusion.3), channel_id=1, source_target_pairs={{0,16},{16,0},{8,24},{24,8},{32,48},{48,32},{40,56},{56,40},{64,80... | collective-permute-start | bytes 5505032 | tf_op jit(solution)/shard_map/ppermute | solution.py:24
  51.8 176.9 %collective-permute-start.3 = (bf16[2,1792,256]{2,1,0:T(8,128)(2,1)}, bf16[2,1792,256]{2,1,0:T(8,128)(2,1)}, u32[]{:S(2)}, u32[]{:S(2)}) collective-permute-start(bf16[2,1792,256]{2,1,0:T(8,128)(2,1)} %maximum_select_fusion.4), channel_id=1, source_target_pairs={{0,16},{16,0},{8,24},{24,8},{32,48},{48,32},{40,56},{56,40},{64,80... | collective-permute-start | bytes 5505032 | tf_op jit(solution)/shard_map/ppermute | solution.py:24
  260.4 70.1 %copy-start.2 = (f32[16,8]{0,1:T(8,128)S(1)}, f32[16,8]{0,1:T(8,128)}, u32[]{:S(2)}) copy-start(f32[16,8]{0,1:T(8,128)} %param.8) | copy-start | bytes 1540
  320.1 26.3 %all-to-all-start.1 = ((bf16[64,4,896]{2,1,0:T(4,128)(2,1)}), bf16[64,4,896]{2,1,0:T(4,128)(2,1)S(1)}, u32[]{:S(2)}, u32[]{:S(2)}) async-start(bf16[64,4,896]{2,1,0:T(4,128)(2,1)} %reshape.89), calls=%async_computation.1 | async-start | bytes 917504 | tf_op jit(solution)/shard_map/all_to_all | solution.py:94
Sparse Core Ops, SparseCore 0:
  260.6 57.3 reduce-scatter.3
where the time goes:
time: 356 us; the launch traced here: 355 us
  waiting for transfers between devices  238 us (67%)
  starting transfers between devices  37.5 us (11%)
  local copies, waits for them, and re-layouts  26.7 us (8%)
  other arithmetic  22.2 us (6%)
  matrix products  17.2 us (5%)
  between operations  13.6 us (4%)
    ppermute x6, waiting for transfers between devices, swapped(): return lax.ppermute(block, axis, route)  165 us
    unnamed x2, waiting for transfers between devices  57.6 us
    select_n x6, other arithmetic, local(): jnp.where(upper, jnp.concatenate([far_piece, near_piece], axis=0), jnp.co...  20.7 us
    all_to_all x1, waiting for transfers between devices, local(): lax.all_to_all(results, 'expert', split_axis=0, concat_axis=0, tiled=True)  15.7 us
    ppermute x6, starting transfers between devices, swapped(): return lax.ppermute(block, axis, route)  15.2 us
    all_to_all x1, starting transfers between devices, local(): lax.all_to_all(outgoing, 'expert', split_axis=0, concat_axis=0, tiled=True)  12 us
    all_to_all x1, starting transfers between devices, local(): lax.all_to_all(results, 'expert', split_axis=0, concat_axis=0, tiled=True)  10.3 us
    dot_general x1, matrix products, expert_rows(): jnp.dot(hidden, full_down, preferred_element_type=jnp.float32)  9.98 us
  transfers between devices with their start and end apart: 9, of which 5 were waited for; matrix products, arithmetic and copies ran while one was open for 7% of the time, Pallas kernels for 0%

commit v1 on v0

v1 whole, which is shorter than its diff:
```python
import jax
import jax.numpy as jnp
from jax import lax
from jax.sharding import PartitionSpec as P

EXPERTS = 16


def local(tokens, routes, route_weights, gate_weight, up_weight, down_weight):
    tok_dev, model_width = tokens.shape
    owners = lax.axis_size("expert")
    splits = lax.axis_size("hsplit")
    group_size = owners // EXPERTS
    slice_width = model_width // group_size
    piece_width = slice_width // splits
    units = gate_weight.shape[2]
    h = lax.axis_index("hsplit")
    groups = [[e * group_size + q for q in range(group_size)] for e in range(EXPERTS)]

    mine = lax.dynamic_slice_in_dim(
        tokens.reshape(tok_dev, group_size, splits, piece_width), h, 1, axis=2
    ).reshape(tok_dev, group_size, piece_width)
    outgoing = jnp.broadcast_to(
        mine.transpose(1, 0, 2)[None], (EXPERTS, group_size, tok_dev, piece_width)
    ).reshape(owners, tok_dev, piece_width)
    arrived = lax.all_to_all(outgoing, "expert", split_axis=0, concat_axis=0, tiled=True)
    arrived = arrived.reshape(owners * tok_dev, piece_width)
    gathered = lax.all_gather(arrived, "hsplit", axis=0)
    both = jnp.concatenate([gate_weight[0], up_weight[0]], axis=1)
    part = sum(
        jnp.dot(
            gathered[s],
            both[s * piece_width : (s + 1) * piece_width],
            preferred_element_type=jnp.float32,
        )
        for s in range(splits)
    )
    total = lax.psum_scatter(
        part.astype(jnp.bfloat16), "expert", scatter_dimension=0, tiled=True, axis_index_groups=groups
    ).astype(jnp.float32)
    hidden = (jax.nn.silu(total[:, :units]) * total[:, units:]).astype(jnp.bfloat16)
    hidden = lax.all_gather(hidden, "expert", axis=0, tiled=True, axis_index_groups=groups)
    partial = jnp.stack(
        [
            jnp.dot(
                hidden,
                down_weight[0][:, s * piece_width : (s + 1) * piece_width],
                preferred_element_type=jnp.float32,
            ).astype(jnp.bfloat16)
            for s in range(splits)
        ]
    )
    summed = lax.psum_scatter(partial, "hsplit", scatter_dimension=0, tiled=False)
    results = summed.reshape(owners, tok_dev, piece_width)
    returned = lax.all_to_all(results, "expert", split_axis=0, concat_axis=0, tiled=True)
    chosen = routes[:, :, None] == jnp.arange(EXPERTS, dtype=jnp.int32)[None, None, :]
    factor = jnp.sum(jnp.where(chosen, route_weights[:, :, None], 0.0), axis=1)
    blocks = returned.reshape(EXPERTS, group_size, tok_dev, piece_width).astype(jnp.float32)
    out = jnp.sum(blocks * factor.T[:, None, :, None], axis=0)
    return out.transpose(1, 0, 2).reshape(tok_dev, group_size * piece_width).astype(jnp.bfloat16)


def solution(mesh):
    placed = (
        P("expert", None),
        P("expert", None),
        P("expert", None),
        P("expert", None, "hsplit"),
        P("expert", None, "hsplit"),
        P("expert", "hsplit", None),
    )
    return jax.shard_map(
        local, mesh=mesh, in_specs=placed, out_specs=P("expert", "hsplit"), check_vma=False
    )
```

time: 356 us -> 232 us (0.65)
  waiting for transfers between devices: 238 us -> 149 us
  blocking collectives: 0 us -> 36 us
  starting transfers between devices: 37.5 us -> 10.4 us
  other arithmetic: 22.2 us -> 1.37 us
  local copies, waits for them, and re-layouts: 26.7 us -> 6.05 us
    ppermute x6 -> x0, waiting for transfers between devices: 165 us -> none  [swapped(): return lax.ppermute(block, axis, route)]
    reduce_scatter x0 -> x2, waiting for transfers between devices: none -> 78.1 us  [the longest x1 54 us: local(): lax.psum_scatter(partial, 'hsplit', scatter_dimension=0, tiled=False)]
    unnamed x2 -> x3, waiting for transfers between devices: 57.6 us -> 0.05 us
    all_gather x0 -> x1, waiting for transfers between devices: none -> 53.6 us  [local(): gathered = lax.all_gather(arrived, 'hsplit', axis=0)]
    all_to_all x0 -> x1, blocking collectives: none -> 28.7 us  [local(): lax.all_to_all(outgoing, 'expert', split_axis=0, concat_axis=0, tiled=True)]
    select_n x7 -> x0, other arithmetic: 20.7 us -> none  [the longest x6 20.7 us: local(): jnp.where(upper, jnp.concatenate([far_piece, near_piece], axis=0), jnp.co...]
    ppermute x6 -> x0, starting transfers between devices: 15.2 us -> none  [swapped(): return lax.ppermute(block, axis, route)]
    reshape x4 -> x1, local copies, waits for them, and re-layouts: 14.8 us -> 1.44 us  [local(): tokens.reshape(tok_dev, group_size, splits, piece_width)]
  transfers between devices with their start and end apart: 9 -> 4, of which waited for: 5 -> 4; matrix products, arithmetic and copies ran while one was open for 7% -> 0% of each run, Pallas kernels for 0% -> 0%
where the time goes in v1:
time: 232 us
  waiting for transfers between devices  149 us (64%)
  blocking collectives  36 us (16%)
  matrix products  15.8 us (7%)
  between operations  13.2 us (6%)
  starting transfers between devices  10.4 us (4%)
  local copies, waits for them, and re-layouts  6.05 us (3%)
    reduce_scatter x1, waiting for transfers between devices, local(): lax.psum_scatter(partial, 'hsplit', scatter_dimension=0, tiled=False)  54 us
    all_gather x1, waiting for transfers between devices, local(): gathered = lax.all_gather(arrived, 'hsplit', axis=0)  53.6 us
    all_to_all x1, blocking collectives, local(): lax.all_to_all(outgoing, 'expert', split_axis=0, concat_axis=0, tiled=True)  28.7 us
    reduce_scatter x1, waiting for transfers between devices, local(): lax.psum_scatter(part.astype(jnp.bfloat16), 'expert', scatter_dimension=0...  24.1 us
    all_to_all x1, waiting for transfers between devices, local(): lax.all_to_all(results, 'expert', split_axis=0, concat_axis=0, tiled=True)  17 us
    all_to_all x1, starting transfers between devices, local(): lax.all_to_all(results, 'expert', split_axis=0, concat_axis=0, tiled=True)  10.3 us
    dot_general x8, matrix products, local(): jnp.dot(hidden, down_weight[0][:, s * piece_width:(s + 1) * piece_width],...  9.45 us
    all_gather x1, blocking collectives, local(): lax.all_gather(hidden, 'expert', axis=0, tiled=True, axis_index_groups=gr...  7.29 us
  transfers between devices with their start and end apart: 4, of which 4 were waited for; matrix products, arithmetic and copies ran while one was open for 0% of the time, Pallas kernels for 0%

profile of v1, /device:TPU:1, one launch (start us, length us, event | category | flops | bytes accessed | tf_op | source)
XLA Modules:
  0.0 231.6 jit_solution(837353395854982719)
XLA Ops:
  6.5 1.4 reshape.18
  8.1 28.7 %all_to_all.10 = bf16[64,16,224]{2,1,0:T(8,128)(2,1)S(1)} all-to-all(bf16[64,16,224]{2,1,0:T(8,128)(2,1)S(1)} %bitcast.98), channel_id=1, replica_groups=mesh['expert'=64,'hsplit'=8] {'expert'}, dimensions={0} | all-to-all | bytes 917504 | tf_op jit(solution)/shard_map/all_to_all | solution.py:26
  36.9 1.0 copy.28
  37.9 53.6 %all-gather.2.cloned.1.call-done = bf16[8,1024,224]{1,2,0:T(8,128)(2,1)} async-done(((bf16[1,1024,224]{1,2,0:T(8,128)(2,1)}), bf16[8,1024,224]{1,2,0:T(8,128)(2,1)}) %all-gather.2.cloned.1.call-update) | async-done | bytes 3670032 | tf_op jit(solution)/shard_map/all_gather | solution.py:28
  91.5 1.6 fusion.17
  93.2 0.5 copy-done.2
  95.2 0.5 fusion.21
  96.6 1.9 add_convert_fusion
  98.5 24.1 %reduce-scatter.3.cloned.1.call-done = bf16[256,512]{1,0:T(8,128)(2,1)} async-done(((bf16[1024,512]{1,0:T(8,128)(2,1)}), bf16[256,512]{1,0:T(8,128)(2,1)}) %reduce-scatter.3.cloned.1.call-update) | async-done | bytes 262160 | tf_op jit(solution)/shard_map/reduce_scatter | solution.py:38
  122.6 1.0 convert_element_type.49
  123.7 7.3 %all_gather.7 = bf16[1024,256]{1,0:T(8,128)(2,1)S(1)} all-gather(bf16[256,256]{1,0:T(8,128)(2,1)S(1)} %fusion.24), channel_id=1, replica_groups={{0,8,16,24},{32,40,48,56},{64,72,80,88},{96,104,112,120},{128,136,144,1..., dimensions={0}, use_global_device_ids=true | all-gather | bytes 655360 | tf_op jit(solution)/shard_map/all_gather | solution.py:42
  131.0 1.1 fusion.1
  132.1 1.2 fusion.3
  133.3 1.2 fusion.5
  134.5 1.2 fusion.7
  135.7 1.2 fusion.9
  136.9 1.2 fusion.11
  138.1 1.2 fusion.13
  139.3 1.2 fusion.15
  140.5 54.0 %reduce-scatter.5.cloned.1.call-done = bf16[1,1024,224]{1,2,0:T(8,128)(2,1)} async-done(((bf16[8,1024,224]{1,2,0:T(8,128)(2,1)}), bf16[1,1024,224]{1,2,0:T(8,128)(2,1)}) %reduce-scatter.5.cloned.1.call-update) | async-done | bytes 458768 | tf_op jit(solution)/shard_map/reduce_scatter | solution.py:53
  194.5 2.0 copy.29
  196.5 10.3 %all-to-all-start.1 = ((bf16[64,16,224]{2,1,0:T(8,128)(2,1)}), bf16[64,16,224]{2,1,0:T(8,128)(2,1)S(1)}, u32[]{:S(2)}, u32[]{:S(2)}) async-start(bf16[64,16,224]{2,1,0:T(8,128)(2,1)} %bitcast.23), calls=%async_computation.3 | async-start | bytes 1048576 | tf_op jit(solution)/shard_map/all_to_all | solution.py:55
  207.2 17.0 %all-to-all-done.1 = bf16[64,16,224]{2,1,0:T(8,128)(2,1)S(1)} async-done(((bf16[64,16,224]{2,1,0:T(8,128)(2,1)}), bf16[64,16,224]{2,1,0:T(8,128)(2,1)S(1)}, u32[]{:S(2)}, u32[]{:S(2)}) %all-to-all-start.1) | async-done | bytes 458784 | tf_op jit(solution)/shard_map/all_to_all | solution.py:55
  224.4 0.7 convert_element_type.63
  (32 shorter events, 3.3 us)
Async XLA Ops:
  6.5 85.0 %copy-start = (bf16[1,1792,256]{2,1,0:T(8,128)(2,1)S(1)}, bf16[1,1792,256]{2,1,0:T(8,128)(2,1)}, u32[]{:S(2)}) copy-start(bf16[1,1792,256]{2,1,0:T(8,128)(2,1)} %param.9) | copy-start | bytes 2752516
  6.5 85.0 %copy-start.1 = (bf16[1,1792,256]{2,1,0:T(8,128)(2,1)S(1)}, bf16[1,1792,256]{2,1,0:T(8,128)(2,1)}, u32[]{:S(2)}) copy-start(bf16[1,1792,256]{2,1,0:T(8,128)(2,1)} %param.10) | copy-start | bytes 2752516
  6.5 85.0 %all-gather.2.cloned.1.call-start = ((), (), s32[]{:S(2)}) async-start(), calls=%async_computation.4 | async-start | bytes 4128768 | tf_op jit(solution)/shard_map/all_gather | solution.py:28
  37.9 84.7 %reduce-scatter.3.cloned.1.call-start = ((), (), s32[]{:S(2)}) async-start(), calls=%async_computation.5 | async-start | bytes 1310720 | tf_op jit(solution)/shard_map/reduce_scatter | solution.py:38
  91.5 2.2 copy-start.2
  98.5 32.6 %copy-start.3 = (bf16[1,256,1792]{2,1,0:T(8,128)(2,1)S(1)}, bf16[1,256,1792]{2,1,0:T(8,128)(2,1)}, u32[]{:S(2)}) copy-start(bf16[1,256,1792]{2,1,0:T(8,128)(2,1)} %param.11) | copy-start | bytes 2752516
  98.5 96.0 %reduce-scatter.5.cloned.1.call-start = ((), (), s32[]{:S(2)}) async-start(), calls=%async_computation.6 | async-start | bytes 4128768 | tf_op jit(solution)/shard_map/reduce_scatter | solution.py:53
  140.5 66.4 %copy-start.4 = (s32[16,8]{0,1:T(8,128)S(1)}, s32[16,8]{0,1:T(8,128)}, u32[]{:S(2)}) copy-start(s32[16,8]{0,1:T(8,128)} %param.7) | copy-start | bytes 1540
  140.5 66.5 %copy-start.5 = (f32[16,8]{0,1:T(8,128)S(1)}, f32[16,8]{0,1:T(8,128)}, u32[]{:S(2)}) copy-start(f32[16,8]{0,1:T(8,128)} %param.8) | copy-start | bytes 1540
  196.5 27.7 %all-to-all-start.1 = ((bf16[64,16,224]{2,1,0:T(8,128)(2,1)}), bf16[64,16,224]{2,1,0:T(8,128)(2,1)S(1)}, u32[]{:S(2)}, u32[]{:S(2)}) async-start(bf16[64,16,224]{2,1,0:T(8,128)(2,1)} %bitcast.23), calls=%async_computation.3 | async-start | bytes 1048576 | tf_op jit(solution)/shard_map/all_to_all | solution.py:55
Sparse Core Ops, SparseCore 0:
  38.0 53.4 all-gather.1
  98.6 23.9 reduce-scatter.2
  140.6 53.8 reduce-scatter.4

commit v2 on v1

v2 whole, which is shorter than its diff:
```python
import jax
import jax.numpy as jnp
from jax import lax
from jax.experimental import pallas as pl
from jax.experimental.pallas import tpu as pltpu
from jax.sharding import PartitionSpec as P

EXPERTS = 16
Q = 4
Z = 8
LX = 4
LY = 4
TOK = 16
D = 7168
W = D // Q
HALF = W // 2
PIECE = W // Z
UNITS = 256
ROWS = EXPERTS * TOK
SUB = ROWS // 2
SHARE = ROWS // Q
BF = jnp.bfloat16
F32 = jnp.float32


def kernel(
    tok, routes, rw, gate_in, up_in, down_in, out,
    xb, wg, wu, wd, dj, acc, pbuf, prec, hid, rsend, rrecv, fin, ret,
    w_sem, g_send, g_recv, y_send, y_recv, x_send, x_recv,
    up_send, up_recv, dn_send, dn_recv,
    p_send, p_recv, h_send, h_recv, rs_send, rs_recv, a_send, a_recv,
):
    p = lax.axis_index("expert")
    z = lax.axis_index("hsplit")
    e, q = p // Q, p % Q
    ex, ey = e // LY, e % LY
    z_up, z_dn = (z + 1) % Z, (z + Z - 1) % Z
    open_sends = []

    def remote(src, dst, send, recv, to_p, to_z):
        return pltpu.make_async_remote_copy(
            src_ref=src, dst_ref=dst, send_sem=send, recv_sem=recv,
            device_id=(to_p, to_z), device_id_type=pl.DeviceIdType.MESH,
        )

    def send(*args):
        copy = remote(*args)
        copy.start()
        open_sends.append(copy)

    def arrived(ref, sem):
        pltpu.make_async_copy(ref, ref, sem).wait()

    loads = [
        pltpu.make_async_copy(src, dst, w_sem.at[i])
        for i, (src, dst) in enumerate(((gate_in, wg), (up_in, wu), (down_in, wd)))
    ]
    for load in loads:
        load.start()

    barrier = pltpu.get_barrier_semaphore()

    def greet(i, carry):
        pl.semaphore_signal(
            barrier, inc=1, device_id=((p + i) % (EXPERTS * Q), z), device_id_type=pl.DeviceIdType.MESH
        )
        return carry

    lax.fori_loop(1, EXPERTS * Q, greet, 0)
    for to_z in (z_up, z_dn):
        pl.semaphore_signal(barrier, inc=1, device_id=(p, to_z), device_id_type=pl.DeviceIdType.MESH)
    pl.semaphore_wait(barrier, EXPERTS * Q + 1)

    mine = xb.at[z, pl.ds(pl.multiple_of(e * TOK, TOK), TOK)]
    shares = q == z // 2

    def share_of(to_q):
        start = pl.multiple_of(to_q * W + (z % 2) * HALF, 128)
        return tok.at[:, pl.ds(start, HALF)]

    g_copies = [
        remote(share_of((q + d) % Q), mine, g_send.at[d - 1], g_recv.at[0], e * Q + (q + d) % Q, z)
        for d in range(1, Q)
    ]
    own_share = pltpu.make_async_copy(share_of(q), mine, g_recv.at[0])

    @pl.when(shares)
    def _():
        for copy in g_copies:
            copy.start()
        own_share.start()

    arrived(mine, g_recv.at[0])
    for d in range(1, LY):
        send(mine, mine, y_send.at[d - 1], y_recv.at[d - 1], (ex * LY + (ey + d) % LY) * Q + q, z)
    for d in range(1, LY):
        arrived(xb.at[z, pl.ds(pl.multiple_of((ex * LY + (ey + LY - d) % LY) * TOK, TOK), TOK)], y_recv.at[d - 1])
    column = LY * TOK
    mine_x = xb.at[z, pl.ds(pl.multiple_of(ex * column, column), column)]
    for d in range(1, LX):
        send(mine_x, mine_x, x_send.at[d - 1], x_recv.at[d - 1], (((ex + d) % LX) * LY + ey) * Q + q, z)
    for load in loads:
        load.wait()
    for d in range(1, LX):
        arrived(
            xb.at[z, pl.ds(pl.multiple_of(((ex + LX - d) % LX) * column, column), column)], x_recv.at[d - 1]
        )

    steps = 7

    def half_of(block, k, way):
        which = k % 2 if way > 0 else (k + 1) % 2
        return xb.at[block, pl.ds(which * SUB, SUB)]

    def ring_send(k, way):
        block = (z - way * (k // 2) + Z) % Z
        ref = half_of(block, k, way)
        if way > 0:
            send(ref, ref, up_send.at[k], up_recv.at[k], p, z_up)
        else:
            send(ref, ref, dn_send.at[k], dn_recv.at[k], p, z_dn)

    def ring_arrived(k, way):
        block = (z - way * (k // 2 + 1) + 2 * Z) % Z
        arrived(half_of(block, k, way), (up_recv if way > 0 else dn_recv).at[k])

    def gate_up(block):
        rows = pl.ds(pl.multiple_of((block % 2) * HALF, 128), HALF)
        x = xb[block]
        return (
            jnp.dot(x, wg[rows, :], preferred_element_type=F32),
            jnp.dot(x, wu[rows, :], preferred_element_type=F32),
        )

    def add_block(block, first):
        a, b = gate_up(block)
        group = block // 2
        if first:
            acc[group, :, :UNITS] = a
            acc[group, :, UNITS:] = b
        else:
            acc[group, :, :UNITS] += a
            acc[group, :, UNITS:] += b

    side = jnp.where(z % 2 == 1, 1, Q - 1)
    own_group = z // 2
    order = (own_group, (own_group + side) % Q, (own_group + 2 * Q - side) % Q, (own_group + 2) % Q)

    def share_partials(i):
        pbuf[i] = acc[order[i]].astype(BF)
        for d in range(1, Q):
            to = (q + d) % Q
            rows = pl.ds(pl.multiple_of(to * SHARE, SHARE), SHARE)
            send(pbuf.at[i, rows], prec.at[i, d - 1], p_send.at[i, d - 1], p_recv.at[i, d - 1], e * Q + to, z)

    def share_hidden(i):
        rows = pl.ds(pl.multiple_of(q * SHARE, SHARE), SHARE)
        total = acc[order[i], rows, :]
        for d in range(1, Q):
            arrived(prec.at[i, d - 1], p_recv.at[i, d - 1])
            total += prec[i, d - 1].astype(F32)
        g, u = total[:, :UNITS], total[:, UNITS:]
        hid[order[i], rows, :] = (g / (1.0 + jnp.exp(-g)) * u).astype(BF)
        ref = hid.at[order[i], rows]
        for d in range(1, Q):
            send(ref, ref, h_send.at[i, d - 1], h_recv.at[i, d - 1], e * Q + (q + d) % Q, z)

    for k in (0, 1):
        ring_send(k, 1)
        ring_send(k, -1)
    add_block(z, True)
    for j in range(Z):
        dj[j] = wd[:, j * PIECE : (j + 1) * PIECE]
    for k in range(steps):
        for way in (1, -1):
            ring_arrived(k, way)
            if k + 2 < steps:
                ring_send(k + 2, way)
        if k == 1:
            partner = jnp.where(z % 2 == 0, z_up, z_dn)
            other = jnp.where(z % 2 == 0, z_dn, z_up)
            add_block(partner, False)
            share_partials(0)
            add_block(other, True)
        elif k == 3:
            closing = jnp.where(z % 2 == 0, (z + Z - 2) % Z, (z + 2) % Z)
            opening = jnp.where(z % 2 == 0, (z + 2) % Z, (z + Z - 2) % Z)
            add_block(closing, False)
            share_partials(1)
            share_hidden(0)
            add_block(opening, True)
        elif k == 5:
            closing = jnp.where(z % 2 == 0, (z + 3) % Z, (z + Z - 3) % Z)
            opening = jnp.where(z % 2 == 0, (z + Z - 3) % Z, (z + 3) % Z)
            add_block(closing, False)
            share_partials(2)
            share_hidden(1)
            add_block(opening, True)
            share_hidden(2)
    add_block((z + 4) % Z, False)
    share_partials(3)
    share_hidden(3)
    for i in range(Q):
        for d in range(1, Q):
            rows = pl.ds(pl.multiple_of(((q + Q - d) % Q) * SHARE, SHARE), SHARE)
            arrived(hid.at[order[i], rows], h_recv.at[i, d - 1])

    def way_of(c):
        return 1 if c < 2 else -1

    def sum_copy(c, s):
        return remote(
            rsend.at[c, s], rrecv.at[c, s], rs_send.at[c, s], rs_recv.at[c, s],
            p, z_up if way_of(c) > 0 else z_dn,
        )

    def term(c, j):
        return jnp.dot(hid[c], dj[j], preferred_element_type=F32)

    for c in (0, 2, 1, 3):
        rsend[c, 0] = term(c, (z - way_of(c) + Z) % Z).astype(BF)
        sum_copy(c, 0).start()

    def sum_step(s, carry):
        for c in (0, 2, 1, 3):
            j = (z - way_of(c) * (1 + s) + 2 * Z) % Z
            value = term(c, j)
            arrived(rrecv.at[c, s - 1], rs_recv.at[c, s - 1])
            rsend[c, s] = (value + rrecv[c, s - 1].astype(F32)).astype(BF)
            sum_copy(c, s).start()
        return carry

    lax.fori_loop(1, Z - 1, sum_step, 0)

    for c in (0, 2, 1, 3):
        value = term(c, z)
        arrived(rrecv.at[c, Z - 2], rs_recv.at[c, Z - 2])
        fin[c] = (value + rrecv[c, Z - 2].astype(F32)).astype(BF)

        def home(i, carry, c=c):
            to_e = (e + i) % EXPERTS
            to = to_e * Q + c
            src = fin.at[c, pl.ds(pl.multiple_of(to_e * TOK, TOK), TOK)]

            @pl.when(to != p)
            def _():
                remote(src, ret.at[p], a_send.at[0], a_recv.at[0], to, z).start()

            @pl.when(to == p)
            def _():
                pltpu.make_async_copy(src, ret.at[p], a_recv.at[0]).start()

            return carry

        lax.fori_loop(0, EXPERTS, home, 0)

    arrived(ret, a_recv.at[0])
    named, share = routes[...], rw[...]
    totals = [jnp.zeros((TOK, PIECE), F32) for _ in range(Q)]
    for x in range(EXPERTS):
        factor = jnp.sum(jnp.where(named == x, share, 0.0), axis=1, keepdims=True)
        for c in range(Q):
            totals[c] += factor * ret[x * Q + c].astype(F32)
    for c in range(Q):
        out[c] = totals[c].astype(BF)

    for copy in open_sends:
        copy.wait_send()

    @pl.when(shares)
    def _():
        for copy in g_copies:
            copy.wait_send()

    for c in range(Q):
        for s in range(Z - 1):
            sum_copy(c, s).wait_send()
    arrived(ret.at[pl.ds(0, EXPERTS * Q - 1)], a_send.at[0])


def local(tokens, routes, route_weights, gate_weight, up_weight, down_weight):
    dma = pltpu.SemaphoreType.DMA
    vmem = pl.BlockSpec(memory_space=pltpu.VMEM)
    anywhere = pl.BlockSpec(memory_space=pl.ANY)
    got = pl.pallas_call(
        kernel,
        out_shape=jax.ShapeDtypeStruct((Q, TOK, PIECE), BF),
        in_specs=[vmem, vmem, vmem, anywhere, anywhere, anywhere],
        out_specs=vmem,
        scratch_shapes=[
            pltpu.VMEM((Z, ROWS, HALF), BF),
            pltpu.VMEM((W, UNITS), BF),
            pltpu.VMEM((W, UNITS), BF),
            pltpu.VMEM((UNITS, W), BF),
            pltpu.VMEM((Z, UNITS, PIECE), BF),
            pltpu.VMEM((Q, ROWS, 2 * UNITS), F32),
            pltpu.VMEM((Q, ROWS, 2 * UNITS), BF),
            pltpu.VMEM((Q, Q - 1, SHARE, 2 * UNITS), BF),
            pltpu.VMEM((Q, ROWS, UNITS), BF),
            pltpu.VMEM((Q, Z - 1, ROWS, PIECE), BF),
            pltpu.VMEM((Q, Z - 1, ROWS, PIECE), BF),
            pltpu.VMEM((Q, ROWS, PIECE), BF),
            pltpu.VMEM((EXPERTS * Q, TOK, PIECE), BF),
            dma((3,)), dma((3,)), dma((1,)), dma((3,)), dma((3,)), dma((3,)), dma((3,)),
            dma((7,)), dma((7,)), dma((7,)), dma((7,)),
            dma((4, 3)), dma((4, 3)), dma((4, 3)), dma((4, 3)),
            dma((4, 7)), dma((4, 7)), dma((1,)), dma((1,)),
        ],
        compiler_params=pltpu.CompilerParams(
            collective_id=0, has_side_effects=True, vmem_limit_bytes=48 * 1024 * 1024
        ),
        cost_estimate=pl.CostEstimate(flops=3 * 10**9, bytes_accessed=4 * 10**6, transcendentals=10**5),
    )(tokens, routes, route_weights, gate_weight[0], up_weight[0], down_weight[0])
    return got.transpose(1, 0, 2).reshape(TOK, Q * PIECE)


def solution(mesh):
    placed = (
        P("expert", None),
        P("expert", None),
        P("expert", None),
        P("expert", None, "hsplit"),
        P("expert", None, "hsplit"),
        P("expert", "hsplit", None),
    )
    return jax.shard_map(
        local, mesh=mesh, in_specs=placed, out_specs=P("expert", "hsplit"), check_vma=False
    )
```

time: 232 us -> 138 us (0.59)
  waiting for transfers between devices: 149 us -> 0 us
  Pallas kernels: 0 us -> 131 us
  blocking collectives: 36 us -> 0 us
  matrix products: 15.8 us -> 0 us
  between operations: 13.2 us -> 0.02 us
  starting transfers between devices: 10.4 us -> 0 us
    pallas_call x0 -> x1, Pallas kernels: none -> 131 us  [local(): pl.pallas_call(kernel, out_shape=jax.ShapeDtypeStruct((Q, TOK, PIECE), BF...]
    reduce_scatter x2 -> x0, waiting for transfers between devices: 78.1 us -> none  [the longest x1 54 us: local(): lax.psum_scatter(partial, 'hsplit', scatter_dimension=0, tiled=False)]
    all_gather x1 -> x0, waiting for transfers between devices: 53.6 us -> none  [local(): gathered = lax.all_gather(arrived, 'hsplit', axis=0)]
    all_to_all x1 -> x0, blocking collectives: 28.7 us -> none  [local(): lax.all_to_all(outgoing, 'expert', split_axis=0, concat_axis=0, tiled=True)]
    all_to_all x1 -> x0, waiting for transfers between devices: 17 us -> none  [local(): lax.all_to_all(results, 'expert', split_axis=0, concat_axis=0, tiled=True)]
    dot_general x16 -> x0, matrix products: 15.8 us -> none  [the longest x8 9.45 us: local(): jnp.dot(hidden, down_weight[0][:, s * piece_width:(s + 1) * piece_width],...]
    all_to_all x1 -> x0, starting transfers between devices: 10.3 us -> none  [local(): lax.all_to_all(results, 'expert', split_axis=0, concat_axis=0, tiled=True)]
    all_gather x1 -> x0, blocking collectives: 7.29 us -> none  [local(): lax.all_gather(hidden, 'expert', axis=0, tiled=True, axis_index_groups=gr...]
  transfers between devices with their start and end apart: 4 -> 0, of which waited for: 4 -> 0; matrix products, arithmetic and copies ran while one was open for 0% -> 0% of each run, Pallas kernels for 0% -> 0%
where the time goes in v2:
time: 138 us
  Pallas kernels  131 us (95%)
  local copies, waits for them, and re-layouts  6.64 us (5%)
    pallas_call x1, Pallas kernels, local(): pl.pallas_call(kernel, out_shape=jax.ShapeDtypeStruct((Q, TOK, PIECE), BF...  131 us
    unnamed x14, local copies, waits for them, and re-layouts  5.92 us

profile of v2, /device:TPU:1, one launch (start us, length us, event | category | flops | bytes accessed | tf_op | source)
XLA Modules:
  0.0 137.9 jit_solution(14990992193965116469)
XLA Ops:
  0.0 0.0 copy-start.4
  0.0 0.7 copy-done.4
  0.7 0.0 copy-start.5
  0.7 0.1 copy.9.routes
  0.8 0.6 copy-done.5
  1.4 0.1 copy.10.rw
  1.4 0.0 copy-start
  1.4 1.2 copy-done
  2.6 0.0 copy-start.1
  2.6 1.2 copy-done.1
  3.8 0.0 copy-start.2
  3.8 1.2 copy-done.2
  5.0 0.0 copy-start.3
  5.0 0.9 copy-done.3
  5.9 131.3 %shard_map.64 = bf16[4,16,224]{2,1,0:T(8,128)(2,1)S(1)} custom-call(bf16[16,7168]{1,0:T(8,128)(2,1)S(1)} %copy-done.3, s32[16,8]{1,0:T(8,128)S(1)} %copy.9.routes, f32[16,8]{1,0:T(8,128)S(1)} %copy.10.rw, bf16[1792,256]{1,0:T(8,128)(2,1)S(1)} %bitcast.5, bf16[1792,256]{1,0:T(8,128)(2,1)S(1)} %bitcast.6, bf16[256,1792]{1,0:T(8,128)(2,1)S(1)} %bitcast.7), custom_call_target="tpu_custom_call" | custom-call | flops 3000000000 | bytes 4000000 | tf_op jit(solution)/shard_map/pallas_call | solution.py:285
  137.2 0.7 reshape.3
  (1 shorter events, 0.0 us)
Async XLA Ops:
  0.0 0.7 copy-start.4
  0.7 0.7 copy-start.5
  1.4 1.2 copy-start
  2.6 1.2 copy-start.1
  3.8 1.2 copy-start.2
  5.0 0.9 copy-start.3

commit v3 on v2

v3 whole, which is shorter than its diff:
```python
import jax
import jax.numpy as jnp
from jax import lax
from jax.experimental import pallas as pl
from jax.experimental.pallas import tpu as pltpu
from jax.sharding import PartitionSpec as P

EXPERTS = 16
Q = 4
Z = 8
TOP = 8
LX = 4
LY = 4
TOK = 16
D = 7168
W = D // Q
PART = 384
REST = W - 2 * PART
PIECE = W // Z
UNITS = 256
ROWS = EXPERTS * TOK
SUB = ROWS // 2
SHARE = ROWS // Q
BF = jnp.bfloat16
F32 = jnp.float32


def kernel(
    tok_in, routes_in, rw_in, gate_in, up_in, down_in, out,
    tok, routes, rw, xb, bb, wg, wu, wd, dj, acc, pbuf, pcore, ybuf, py, hid, rsend, rrecv, fin, ret,
    w_sem, g_send, g_recv, b_send, b_recv, x_send, x_recv, y_send, y_recv, bx_send, bx_recv,
    up_send, up_recv, dn_send, dn_recv,
    p_send, p_recv, m_send, m_recv, h_send, h_recv, rs_send, rs_recv, a_send, a_recv,
):
    p = lax.axis_index("expert")
    z = lax.axis_index("hsplit")
    e, q = p // Q, p % Q
    ex, ey = e // LY, e % LY
    z_up, z_dn = (z + 1) % Z, (z + Z - 1) % Z
    open_sends = []

    def remote(src, dst, send, recv, to_p, to_z):
        return pltpu.make_async_remote_copy(
            src_ref=src, dst_ref=dst, send_sem=send, recv_sem=recv,
            device_id=(to_p, to_z), device_id_type=pl.DeviceIdType.MESH,
        )

    def send(*args):
        copy = remote(*args)
        copy.start()
        open_sends.append(copy)

    def arrived(ref, sem):
        pltpu.make_async_copy(ref, ref, sem).wait()

    def owner(x, y, k):
        return (x * LY + y) * Q + k

    def rows(start, count):
        return pl.ds(pl.multiple_of(start, 16), count)

    pairs = ((tok_in, tok), (gate_in, wg), (up_in, wu), (down_in, wd), (routes_in, routes), (rw_in, rw))
    loads = [pltpu.make_async_copy(src, dst, w_sem.at[i]) for i, (src, dst) in enumerate(pairs)]
    for load in loads:
        load.start()

    barrier = pltpu.get_barrier_semaphore()

    def greet(i, carry):
        pl.semaphore_signal(
            barrier, inc=1, device_id=((p + i) % (EXPERTS * Q), z), device_id_type=pl.DeviceIdType.MESH
        )
        return carry

    lax.fori_loop(1, EXPERTS * Q, greet, 0)
    for to_z in (z_up, z_dn):
        pl.semaphore_signal(barrier, inc=1, device_id=(p, to_z), device_id_type=pl.DeviceIdType.MESH)
    loads[0].wait()
    pl.semaphore_wait(barrier, EXPERTS * Q + 1)

    side = jnp.where(z % 2 == 1, 1, Q - 1)
    own_group = z // 2
    order = (own_group, (own_group + side) % Q, (own_group + 2 * Q - side) % Q, (own_group + 2) % Q)
    column = LY * TOK
    own_rows = rows(e * TOK, TOK)

    mine = xb.at[z, own_rows]
    shares = q == z // 2

    def share_of(to_q):
        return tok.at[:, pl.ds(pl.multiple_of(to_q * W + (z % 2) * PART, 128), PART)]

    g_copies = [
        remote(
            share_of((q + d % Q) % Q), mine, g_send.at[d], g_recv.at[0],
            owner(ex, (ey + d // Q) % LY, (q + d % Q) % Q), z,
        )
        for d in range(1, Q * LY)
    ]
    own_share = pltpu.make_async_copy(share_of(q), mine, g_recv.at[0])

    def rest_of(to_q):
        return tok.at[:, pl.ds(pl.multiple_of(to_q * W + 2 * PART, 128), REST)]

    own_rest = pltpu.make_async_copy(rest_of(q), bb.at[q, own_rows], b_recv.at[0])
    for d in range(1, Q):
        to = (q + d) % Q
        send(rest_of(to), bb.at[q, own_rows], b_send.at[d], b_recv.at[d], e * Q + to, z)
    own_rest.start()

    @pl.when(shares)
    def _():
        for copy in g_copies:
            copy.start()
        own_share.start()

    own_rest.wait()
    for d in range(1, Q):
        arrived(bb.at[(q + Q - d) % Q, own_rows], b_recv.at[d])

    def y_sends(i):
        ref = bb.at[order[i], own_rows]
        for d in (1, 3, 2):
            send(ref, ref, y_send.at[i, d], y_recv.at[i, d], owner(ex, (ey + d) % LY, q), z)

    def y_arrived(i):
        for d in (1, 3, 2):
            arrived(bb.at[order[i], rows((ex * LY + (ey + LY - d) % LY) * TOK, TOK)], y_recv.at[i, d])

    x_up, x_dn = (ex + 1) % LX, (ex + LX - 1) % LX
    x_far = (ex + 2) % LX

    def x_sends(i):
        ref = bb.at[order[i], rows(ex * column, column)]
        send(ref, ref, bx_send.at[i, 0], bx_recv.at[i, 0], owner(x_up, ey, q), z)
        send(ref, ref, bx_send.at[i, 1], bx_recv.at[i, 1], owner(x_dn, ey, q), z)

    def x_forward(i):
        half = column // 2
        arrived(bb.at[order[i], rows(x_dn * column, column)], bx_recv.at[i, 0])
        ref = bb.at[order[i], rows(x_dn * column, half)]
        send(ref, ref, bx_send.at[i, 2], bx_recv.at[i, 2], owner(x_up, ey, q), z)
        arrived(bb.at[order[i], rows(x_up * column, column)], bx_recv.at[i, 1])
        ref = bb.at[order[i], rows(x_up * column + half, half)]
        send(ref, ref, bx_send.at[i, 3], bx_recv.at[i, 3], owner(x_dn, ey, q), z)

    def x_arrived(i):
        half = column // 2
        arrived(bb.at[order[i], rows(x_far * column, half)], bx_recv.at[i, 2])
        arrived(bb.at[order[i], rows(x_far * column + half, half)], bx_recv.at[i, 3])

    y_sends(0)
    mine_x = xb.at[z, rows(ex * column, column)]
    arrived(mine_x, g_recv.at[0])
    for d in range(1, LX):
        send(mine_x, mine_x, x_send.at[d], x_recv.at[d], owner((ex + d) % LX, ey, q), z)
    for i in range(1, Q):
        y_sends(i)
    for load in loads[1:]:
        load.wait()
    y_arrived(0)
    x_sends(0)
    for d in range(1, LX):
        arrived(xb.at[z, rows(((ex + LX - d) % LX) * column, column)], x_recv.at[d])

    steps = 7

    def half_of(block, k, way):
        which = k % 2 if way > 0 else (k + 1) % 2
        return xb.at[block, pl.ds(which * SUB, SUB)]

    def ring_send(k, way):
        block = (z - way * (k // 2) + Z) % Z
        ref = half_of(block, k, way)
        if way > 0:
            send(ref, ref, up_send.at[k], up_recv.at[k], p, z_up)
        else:
            send(ref, ref, dn_send.at[k], dn_recv.at[k], p, z_dn)

    def ring_step(k):
        for way in (1, -1):
            block = (z - way * (k // 2 + 1) + 2 * Z) % Z
            arrived(half_of(block, k, way), (up_recv if way > 0 else dn_recv).at[k])
            if k + 2 < steps:
                ring_send(k + 2, way)

    def add_terms(group, x, wrows, first):
        for at, w in ((0, wg), (UNITS, wu)):
            value = jnp.dot(x, w[wrows, :], preferred_element_type=F32)
            if first:
                acc[group, :, at : at + UNITS] = value
            else:
                acc[group, :, at : at + UNITS] += value

    def add_block(block, first):
        add_terms(block // 2, xb[block], pl.ds(pl.multiple_of((block % 2) * PART, 128), PART), first)

    def add_rest(i):
        x_arrived(i)
        add_terms(order[i], bb[order[i]], pl.ds(2 * PART, REST), False)

    core, chip = q % 2, q // 2

    def share_row(k):
        return (k % 2) * 2 * SHARE + (k // 2) * SHARE

    def share_partials(i):
        pbuf[i] = acc[order[i], rows((1 - core) * 2 * SHARE, 2 * SHARE), :].astype(BF)
        send(pbuf.at[i], pcore.at[i], p_send.at[i], p_recv.at[i], e * Q + chip * 2 + 1 - core, z)

    def cross(i):
        far, near = rows((1 - chip) * SHARE, SHARE), rows(chip * SHARE, SHARE)
        far_row = core * 2 * SHARE + (1 - chip) * SHARE
        arrived(pcore.at[i], p_recv.at[i])
        ybuf[i] = (acc[order[i], rows(far_row, SHARE), :] + pcore[i, far, :].astype(F32)).astype(BF)
        send(ybuf.at[i], py.at[i], m_send.at[i], m_recv.at[i], e * Q + (1 - chip) * 2 + core, z)
        acc[order[i], rows(share_row(q), SHARE), :] += pcore[i, near, :].astype(F32)

    def share_hidden(i):
        here = rows(share_row(q), SHARE)
        arrived(py.at[i], m_recv.at[i])
        total = acc[order[i], here, :] + py[i].astype(F32)
        g, u = total[:, :UNITS], total[:, UNITS:]
        hid[order[i], here, :] = (g / (1.0 + jnp.exp(-g)) * u).astype(BF)
        ref = hid.at[order[i], here]
        for d in range(1, Q):
            send(ref, ref, h_send.at[i, d], h_recv.at[i, d], e * Q + (q + d) % Q, z)

    even = z % 2 == 0

    def nth(up, down):
        return jnp.where(even, (z + up) % Z, (z + down) % Z)

    for k in (0, 1):
        ring_send(k, 1)
        ring_send(k, -1)
    add_block(z, True)
    for j in range(Z):
        dj[j] = wd[:, j * PIECE : (j + 1) * PIECE]
    y_arrived(1)
    x_sends(1)
    ring_step(0)
    x_forward(0)
    ring_step(1)
    add_block(nth(1, Z - 1), False)
    add_rest(0)
    share_partials(0)
    y_arrived(2)
    x_sends(2)
    ring_step(2)
    x_forward(1)
    add_block(nth(Z - 1, 1), True)
    cross(0)
    ring_step(3)
    add_block(nth(Z - 2, 2), False)
    add_rest(1)
    share_partials(1)
    share_hidden(0)
    y_arrived(3)
    x_sends(3)
    ring_step(4)
    x_forward(2)
    add_block(nth(2, Z - 2), True)
    cross(1)
    ring_step(5)
    add_block(nth(3, Z - 3), False)
    add_rest(2)
    share_partials(2)
    share_hidden(1)
    x_forward(3)
    add_block(nth(Z - 3, 3), True)
    cross(2)
    ring_step(6)
    add_block((z + 4) % Z, False)
    share_hidden(2)
    add_rest(3)
    share_partials(3)
    cross(3)
    share_hidden(3)
    for i in range(Q):
        for d in range(1, Q):
            arrived(hid.at[order[i], rows(share_row((q + Q - d) % Q), SHARE)], h_recv.at[i, d])

    def way_of(c):
        return 1 if c < 2 else -1

    def sum_copy(c, s):
        return remote(
            rsend.at[c, s], rrecv.at[c, s], rs_send.at[c, s], rs_recv.at[c, s],
            p, z_up if way_of(c) > 0 else z_dn,
        )

    def term(c, j):
        return jnp.dot(hid[c], dj[j], preferred_element_type=F32)

    for c in (0, 2, 1, 3):
        rsend[c, 0] = term(c, (z - way_of(c) + Z) % Z).astype(BF)
        sum_copy(c, 0).start()

    def sum_step(s, carry):
        for c in (0, 2, 1, 3):
            j = (z - way_of(c) * (1 + s) + 2 * Z) % Z
            value = term(c, j)
            arrived(rrecv.at[c, s - 1], rs_recv.at[c, s - 1])
            rsend[c, s] = (value + rrecv[c, s - 1].astype(F32)).astype(BF)
            sum_copy(c, s).start()
        return carry

    lax.fori_loop(1, Z - 1, sum_step, 0)

    for c in (0, 2, 1, 3):
        value = term(c, z)
        arrived(rrecv.at[c, Z - 2], rs_recv.at[c, Z - 2])
        fin[c] = (value + rrecv[c, Z - 2].astype(F32)).astype(BF)

        def home(i, carry, c=c):
            to_e = (e + i) % EXPERTS
            to = to_e * Q + c
            src = fin.at[c, pl.ds(pl.multiple_of(to_e * TOK, TOK), TOK)]

            @pl.when(to != p)
            def _():
                remote(src, ret.at[p], a_send.at[0], a_recv.at[0], to, z).start()

            @pl.when(to == p)
            def _():
                pltpu.make_async_copy(src, ret.at[p], a_recv.at[0]).start()

            return carry

        lax.fori_loop(0, EXPERTS, home, 0)

    arrived(ret, a_recv.at[0])
    named, share = routes[...], rw[...]
    lane = lax.broadcasted_iota(jnp.int32, (TOK, TOK), 1)
    diagonal = lane == lax.broadcasted_iota(jnp.int32, (TOK, TOK), 0)
    totals = [jnp.zeros((TOK, PIECE), F32) for _ in range(Q)]
    for x in range(EXPERTS):
        row = jnp.sum(jnp.where(named == x, share, 0.0), axis=0, keepdims=True)
        factor = jnp.sum(jnp.where(diagonal, row, 0.0), axis=1, keepdims=True)
        for c in range(Q):
            totals[c] += factor * ret[x * Q + c].astype(F32)
    for c in range(Q):
        out[c] = totals[c].astype(BF)

    for copy in open_sends:
        copy.wait_send()

    @pl.when(shares)
    def _():
        for copy in g_copies:
            copy.wait_send()

    for c in range(Q):
        for s in range(Z - 1):
            sum_copy(c, s).wait_send()
    arrived(ret.at[pl.ds(0, EXPERTS * Q - 1)], a_send.at[0])


def local(tokens, routes, route_weights, gate_weight, up_weight, down_weight):
    dma = pltpu.SemaphoreType.DMA
    vmem = pl.BlockSpec(memory_space=pltpu.VMEM)
    anywhere = pl.BlockSpec(memory_space=pl.ANY)
    got = pl.pallas_call(
        kernel,
        out_shape=jax.ShapeDtypeStruct((Q, TOK, PIECE), BF),
        in_specs=[anywhere] * 6,
        out_specs=vmem,
        scratch_shapes=[
            pltpu.VMEM((TOK, D), BF),
            pltpu.VMEM((TOP, TOK), jnp.int32),
            pltpu.VMEM((TOP, TOK), F32),
            pltpu.VMEM((Z, ROWS, PART), BF),
            pltpu.VMEM((Q, ROWS, REST), BF),
            pltpu.VMEM((W, UNITS), BF),
            pltpu.VMEM((W, UNITS), BF),
            pltpu.VMEM((UNITS, W), BF),
            pltpu.VMEM((Z, UNITS, PIECE), BF),
            pltpu.VMEM((Q, ROWS, 2 * UNITS), F32),
            pltpu.VMEM((Q, 2 * SHARE, 2 * UNITS), BF),
            pltpu.VMEM((Q, 2 * SHARE, 2 * UNITS), BF),
            pltpu.VMEM((Q, SHARE, 2 * UNITS), BF),
            pltpu.VMEM((Q, SHARE, 2 * UNITS), BF),
            pltpu.VMEM((Q, ROWS, UNITS), BF),
            pltpu.VMEM((Q, Z - 1, ROWS, PIECE), BF),
            pltpu.VMEM((Q, Z - 1, ROWS, PIECE), BF),
            pltpu.VMEM((Q, ROWS, PIECE), BF),
            pltpu.VMEM((EXPERTS * Q, TOK, PIECE), BF),
            dma((6,)), dma((16,)), dma((1,)), dma((4,)), dma((4,)), dma((4,)), dma((4,)),
            dma((4, 4)), dma((4, 4)), dma((4, 4)), dma((4, 4)),
            dma((7,)), dma((7,)), dma((7,)), dma((7,)),
            dma((4,)), dma((4,)), dma((4,)), dma((4,)), dma((4, 4)), dma((4, 4)),
            dma((4, 7)), dma((4, 7)), dma((1,)), dma((1,)),
        ],
        compiler_params=pltpu.CompilerParams(
            collective_id=0, has_side_effects=True, vmem_limit_bytes=60 * 1024 * 1024
        ),
        cost_estimate=pl.CostEstimate(flops=3 * 10**9, bytes_accessed=4 * 10**6, transcendentals=10**5),
    )(tokens, routes.T, route_weights.T, gate_weight[0], up_weight[0], down_weight[0])
    return got.transpose(1, 0, 2).reshape(TOK, Q * PIECE)


def solution(mesh):
    placed = (
        P("expert", None),
        P("expert", None),
        P("expert", None),
        P("expert", None, "hsplit"),
        P("expert", None, "hsplit"),
        P("expert", "hsplit", None),
    )
    return jax.shard_map(
        local, mesh=mesh, in_specs=placed, out_specs=P("expert", "hsplit"), check_vma=False
    )
```

time: 138 us -> 122 us (0.88)
  Pallas kernels: 131 us -> 120 us
  local copies, waits for them, and re-layouts: 6.64 us -> 1.48 us
    pallas_call x1, Pallas kernels: 131 us -> 120 us  [local(): pl.pallas_call(kernel, out_shape=jax.ShapeDtypeStruct((Q, TOK, PIECE), BF...]
    unnamed x14 -> x0, local copies, waits for them, and re-layouts: 5.92 us -> none
where the time goes in v3:
time: 122 us; the launch traced here: 121 us
  Pallas kernels  120 us (98%)
  local copies, waits for them, and re-layouts  1.48 us (1%)
    pallas_call x1, Pallas kernels, local(): pl.pallas_call(kernel, out_shape=jax.ShapeDtypeStruct((Q, TOK, PIECE), BF...  120 us

profile of v3, /device:TPU:1, one launch (start us, length us, event | category | flops | bytes accessed | tf_op | source)
XLA Modules:
  0.0 121.1 jit_solution(7116795891640325486)
XLA Ops:
  0.0 119.6 %shard_map.64 = bf16[4,16,224]{2,1,0:T(8,128)(2,1)} custom-call(bf16[16,7168]{1,0:T(8,128)(2,1)} %tok_in.1, s32[8,16]{1,0:T(8,128)} %bitcast.10, f32[8,16]{1,0:T(8,128)} %bitcast.11, bf16[1792,256]{1,0:T(8,128)(2,1)} %bitcast.7, bf16[1792,256]{1,0:T(8,128)(2,1)} %bitcast.8, bf16[256,1792]{1,0:T(8,128)(2,1)} %bitcast.9), custom_call_target="tpu_custom_call" | custom-call | flops 3000000000 | bytes 4000000 | tf_op jit(solution)/shard_map/pallas_call | solution.py:364
  119.6 0.8 copy.7
  120.4 0.7 reshape.3

commit v4 on v3

--- a/solution.py
+++ b/solution.py
@@ -27,10 +27,12 @@
 
 def kernel(
     tok_in, routes_in, rw_in, gate_in, up_in, down_in, out,
-    tok, routes, rw, xb, bb, wg, wu, wd, dj, acc, pbuf, pcore, ybuf, py, hid, rsend, rrecv, fin, ret,
+    tok, routes, rw, xb, bb, wg, wu, wd, dj, acc, pbuf, pcore, ybuf, py, hid,
+    fmat, wbuf, rsend, rrecv, fin, ret, tx1, rx1, tx2, rx2, ty, ry, tz, rz,
     w_sem, g_send, g_recv, b_send, b_recv, x_send, x_recv, y_send, y_recv, bx_send, bx_recv,
     up_send, up_recv, dn_send, dn_recv,
     p_send, p_recv, m_send, m_recv, h_send, h_recv, rs_send, rs_recv, a_send, a_recv,
+    f_send, f_recv, r1_send, r1_recv, r2_send, r2_recv, ry_send, ry_recv, rz_send, rz_recv,
 ):
     p = lax.axis_index("expert")
     z = lax.axis_index("hsplit")
@@ -59,7 +61,7 @@
     def rows(start, count):
         return pl.ds(pl.multiple_of(start, 16), count)
 
-    pairs = ((tok_in, tok), (gate_in, wg), (up_in, wu), (down_in, wd), (routes_in, routes), (rw_in, rw))
+    pairs = ((tok_in, tok), (routes_in, routes), (rw_in, rw), (gate_in, wg), (up_in, wu), (down_in, wd))
     loads = [pltpu.make_async_copy(src, dst, w_sem.at[i]) for i, (src, dst) in enumerate(pairs)]
     for load in loads:
         load.start()
@@ -73,10 +75,28 @@
         return carry
 
     lax.fori_loop(1, EXPERTS * Q, greet, 0)
-    for to_z in (z_up, z_dn):
-        pl.semaphore_signal(barrier, inc=1, device_id=(p, to_z), device_id_type=pl.DeviceIdType.MESH)
-    loads[0].wait()
-    pl.semaphore_wait(barrier, EXPERTS * Q + 1)
+
+    def greet_z(i, carry):
+        pl.semaphore_signal(
+            barrier, inc=1, device_id=(e * Q + i % Q, (z + i // Q) % Z), device_id_type=pl.DeviceIdType.MESH
+        )
+        return carry
+
+    lax.fori_loop(Q, Z * Q, greet_z, 0)
+    for load in loads[:3]:
+        load.wait()
+
+    named, share = routes[...], rw[...]
+    lane = lax.broadcasted_iota(jnp.int32, (TOK, TOK), 1)
+    diagonal = lane == lax.broadcasted_iota(jnp.int32, (TOK, TOK), 0)
+    wide = lax.broadcasted_iota(jnp.int32, (TOK, 128), 1)
+    factors = jnp.zeros((TOK, 128), F32)
+    for x in range(EXPERTS):
+        row = jnp.sum(jnp.where(named == x, share, 0.0), axis=0, keepdims=True)
+        factor = jnp.sum(jnp.where(diagonal, row, 0.0), axis=1, keepdims=True)
+        factors = jnp.where(wide == x, factor, factors)
+    fmat[...] = factors
+    pl.semaphore_wait(barrier, EXPERTS * Q - 1 + (Z - 1) * Q)
 
     side = jnp.where(z % 2 == 1, 1, Q - 1)
     own_group = z // 2
@@ -156,7 +176,23 @@
         send(mine_x, mine_x, x_send.at[d], x_recv.at[d], owner((ex + d) % LX, ey, q), z)
     for i in range(1, Q):
         y_sends(i)
-    for load in loads[1:]:
+
+    def share_factors(i, carry):
+        to = (e + i) % EXPERTS * Q + share_of_column
+
+        @pl.when(to != p)
+        def _():
+            remote(fmat, wbuf.at[q, ey], f_send.at[i], f_recv.at[0], to, z).start()
+
+        @pl.when(to == p)
+        def _():
+            pltpu.make_async_copy(fmat, wbuf.at[q, ey], f_recv.at[0]).start()
+
+        return carry
+
+    share_of_column = (ex % 2) * 2 + ex // 2
+    lax.fori_loop(0, EXPERTS, share_factors, 0)
+    for load in loads[3:]:
         load.wait()
     y_arrived(0)
     x_sends(0)
@@ -221,7 +257,12 @@
         arrived(py.at[i], m_recv.at[i])
         total = acc[order[i], here, :] + py[i].astype(F32)
         g, u = total[:, :UNITS], total[:, UNITS:]
-        hid[order[i], here, :] = (g / (1.0 + jnp.exp(-g)) * u).astype(BF)
+        if i == 0:
+            arrived(wbuf, f_recv.at[0])
+        factor = wbuf[order[i]].reshape(SHARE, 128)
+        at_expert = lax.broadcasted_iota(jnp.int32, (SHARE, 128), 1) == e
+        factor = jnp.sum(jnp.where(at_expert, factor, 0.0), axis=1, keepdims=True)
+        hid[order[i], here, :] = (g / (1.0 + jnp.exp(-g)) * u * factor).astype(BF)
         ref = hid.at[order[i], here]
         for d in range(1, Q):
             send(ref, ref, h_send.at[i, d], h_recv.at[i, d], e * Q + (q + d) % Q, z)
@@ -281,6 +322,8 @@
         for d in range(1, Q):
             arrived(hid.at[order[i], rows(share_row((q + Q - d) % Q), SHARE)], h_recv.at[i, d])
 
+    chunks = (0, 2, 1, 3)
+
     def way_of(c):
         return 1 if c < 2 else -1
 
@@ -291,32 +334,27 @@
         )
 
     def term(c, j):
-        return jnp.dot(hid[c], dj[j], preferred_element_type=F32)
-
-    for c in (0, 2, 1, 3):
-        rsend[c, 0] = term(c, (z - way_of(c) + Z) % Z).astype(BF)
-        sum_copy(c, 0).start()
-
-    def sum_step(s, carry):
-        for c in (0, 2, 1, 3):
+        return jnp.dot(hid[c // 2, c % 2 * SUB : (c % 2 + 1) * SUB, :], dj[j], preferred_element_type=F32)
+
+    def sum_step(s):
+        for c in chunks:
             j = (z - way_of(c) * (1 + s) + 2 * Z) % Z
             value = term(c, j)
-            arrived(rrecv.at[c, s - 1], rs_recv.at[c, s - 1])
-            rsend[c, s] = (value + rrecv[c, s - 1].astype(F32)).astype(BF)
+            if s > 0:
+                arrived(rrecv.at[c, s - 1], rs_recv.at[c, s - 1])
+                value += rrecv[c, s - 1].astype(F32)
+            rsend[c, s] = value.astype(BF)
             sum_copy(c, s).start()
-        return carry
-
-    lax.fori_loop(1, Z - 1, sum_step, 0)
-
-    for c in (0, 2, 1, 3):
+
+    def sum_last(c):
         value = term(c, z)
         arrived(rrecv.at[c, Z - 2], rs_recv.at[c, Z - 2])
         fin[c] = (value + rrecv[c, Z - 2].astype(F32)).astype(BF)
 
-        def home(i, carry, c=c):
-            to_e = (e + i) % EXPERTS
-            to = to_e * Q + c
-            src = fin.at[c, pl.ds(pl.multiple_of(to_e * TOK, TOK), TOK)]
+        def home(i, carry):
+            to_e = c % 2 * (EXPERTS // 2) + (e + i) % (EXPERTS // 2)
+            to = to_e * Q + c // 2
+            src = fin.at[c, rows((e + i) % (EXPERTS // 2) * TOK, TOK)]
 
             @pl.when(to != p)
             def _():
@@ -328,20 +366,100 @@
 
             return carry
 
-        lax.fori_loop(0, EXPERTS, home, 0)
-
-    arrived(ret, a_recv.at[0])
-    named, share = routes[...], rw[...]
-    lane = lax.broadcasted_iota(jnp.int32, (TOK, TOK), 1)
-    diagonal = lane == lax.broadcasted_iota(jnp.int32, (TOK, TOK), 0)
-    totals = [jnp.zeros((TOK, PIECE), F32) for _ in range(Q)]
-    for x in range(EXPERTS):
-        row = jnp.sum(jnp.where(named == x, share, 0.0), axis=0, keepdims=True)
-        factor = jnp.sum(jnp.where(diagonal, row, 0.0), axis=1, keepdims=True)
-        for c in range(Q):
-            totals[c] += factor * ret[x * Q + c].astype(F32)
-    for c in range(Q):
-        out[c] = totals[c].astype(BF)
+        lax.fori_loop(0, EXPERTS // 2, home, 0)
+
+    half = column // 2
+
+    def full_term(t, x):
+        return jnp.dot(hid[2 + t, rows(x * column, column), :], wd[...], preferred_element_type=F32)
+
+    def plane_far(t):
+        tx1[t] = full_term(t, x_far).astype(BF)
+        send(tx1.at[t, :half], rx1.at[t, 0], r1_send.at[t, 0], r1_recv.at[t, 0], owner(x_up, ey, q), z)
+        send(tx1.at[t, half:], rx1.at[t, 1], r1_send.at[t, 1], r1_recv.at[t, 1], owner(x_dn, ey, q), z)
+
+    def plane_near(t):
+        for w, x in ((0, x_up), (1, x_dn)):
+            value = full_term(t, x)
+            mid, rest = slice(w * half, w * half + half), slice((1 - w) * half, (1 - w) * half + half)
+            tx2[t, w, rest, :] = value[rest].astype(BF)
+            arrived(rx1.at[t, w], r1_recv.at[t, w])
+            tx2[t, w, mid, :] = (value[mid] + rx1[t, w].astype(F32)).astype(BF)
+            send(tx2.at[t, w], rx2.at[t, w], r2_send.at[t, w], r2_recv.at[t, w], owner(x, ey, q), z)
+
+    def plane_y(t):
+        value = full_term(t, ex)
+        for w in (0, 1):
+            arrived(rx2.at[t, w], r2_recv.at[t, w])
+            value += rx2[t, w].astype(F32)
+        ty[t] = value.astype(BF)
+        for d in (1, 3, 2):
+            to = (ey + d) % LY
+            send(
+                ty.at[t, rows(to * TOK, TOK)], ry.at[t, d - 1], ry_send.at[t, d - 1], ry_recv.at[t, d - 1],
+                owner(ex, to, q), z,
+            )
+
+    def home_copy(t, j):
+        return remote(tz.at[t, j], rz.at[q, z], rz_send.at[t, j], rz_recv.at[0], e * Q + 2 + t, j)
+
+    def is_here(t, j):
+        return jnp.logical_and(q == 2 + t, z == j)
+
+    def plane_home(t):
+        value = ty[t, rows(ey * TOK, TOK), :].astype(F32)
+        for d in (1, 3, 2):
+            arrived(ry.at[t, d - 1], ry_recv.at[t, d - 1])
+            value += ry[t, d - 1].astype(F32)
+        for j in range(Z):
+            tz[t, j] = value[:, j * PIECE : (j + 1) * PIECE].astype(BF)
+        for j in range(Z):
+
+            @pl.when(jnp.logical_not(is_here(t, j)))
+            def _(j=j):
+                home_copy(t, j).start()
+
+            @pl.when(is_here(t, j))
+            def _(j=j):
+                pltpu.make_async_copy(tz.at[t, j], rz.at[q, z], rz_recv.at[0]).start()
+
+    sum_step(0)
+    plane_far(0)
+    plane_far(1)
+    sum_step(1)
+    plane_near(0)
+    sum_step(2)
+    plane_near(1)
+    sum_step(3)
+    sum_step(4)
+    plane_y(0)
+    sum_step(5)
+    plane_y(1)
+    sum_step(6)
+    plane_home(0)
+    for c in chunks:
+        sum_last(c)
+    plane_home(1)
+
+    @pl.when(q < 2)
+    def _():
+        arrived(ret, a_recv.at[0])
+        for k in range(Q):
+            total = ret[k].astype(F32)
+            for x in range(1, EXPERTS):
+                total += ret[x * Q + k].astype(F32)
+            out[k] = total.astype(BF)
+        arrived(ret.at[pl.ds(0, 2 * EXPERTS - 1)], a_send.at[0])
+
+    @pl.when(q >= 2)
+    def _():
+        arrived(rz, rz_recv.at[0])
+        for k in range(Q):
+            total = rz[k, 0].astype(F32)
+            for j in range(1, Z):
+                total += rz[k, j].astype(F32)
+            out[k] = total.astype(BF)
+        arrived(ret.at[pl.ds(0, 2 * EXPERTS)], a_send.at[0])
 
     for copy in open_sends:
         copy.wait_send()
@@ -351,10 +469,25 @@
         for copy in g_copies:
             copy.wait_send()
 
+    def factors_sent(i, carry):
+        to = (e + i) % EXPERTS * Q + share_of_column
+
+        @pl.when(to != p)
+        def _():
+            remote(fmat, wbuf.at[q, ey], f_send.at[i], f_recv.at[0], to, z).wait_send()
+
+        return carry
+
+    lax.fori_loop(0, EXPERTS, factors_sent, 0)
     for c in range(Q):
         for s in range(Z - 1):
             sum_copy(c, s).wait_send()
-    arrived(ret.at[pl.ds(0, EXPERTS * Q - 1)], a_send.at[0])
+    for t in range(2):
+        for j in range(Z):
+
+            @pl.when(jnp.logical_not(is_here(t, j)))
+            def _(t=t, j=j):
+                home_copy(t, j).wait_send()
 
 
 def local(tokens, routes, route_weights, gate_weight, up_weight, down_weight):
@@ -382,15 +515,27 @@
             pltpu.VMEM((Q, SHARE, 2 * UNITS), BF),
             pltpu.VMEM((Q, SHARE, 2 * UNITS), BF),
             pltpu.VMEM((Q, ROWS, UNITS), BF),
-            pltpu.VMEM((Q, Z - 1, ROWS, PIECE), BF),
-            pltpu.VMEM((Q, Z - 1, ROWS, PIECE), BF),
-            pltpu.VMEM((Q, ROWS, PIECE), BF),
+            pltpu.VMEM((TOK, 128), F32),
+            pltpu.VMEM((Q, LY, TOK, 128), F32),
+            pltpu.VMEM((Q, Z - 1, SUB, PIECE), BF),
+            pltpu.VMEM((Q, Z - 1, SUB, PIECE), BF),
+            pltpu.VMEM((Q, SUB, PIECE), BF),
             pltpu.VMEM((EXPERTS * Q, TOK, PIECE), BF),
+            pltpu.VMEM((2, SHARE, W), BF),
+            pltpu.VMEM((2, 2, SHARE // 2, W), BF),
+            pltpu.VMEM((2, 2, SHARE, W), BF),
+            pltpu.VMEM((2, 2, SHARE, W), BF),
+            pltpu.VMEM((2, SHARE, W), BF),
+            pltpu.VMEM((2, LY - 1, TOK, W), BF),
+            pltpu.VMEM((2, Z, TOK, PIECE), BF),
+            pltpu.VMEM((Q, Z, TOK, PIECE), BF),
             dma((6,)), dma((16,)), dma((1,)), dma((4,)), dma((4,)), dma((4,)), dma((4,)),
             dma((4, 4)), dma((4, 4)), dma((4, 4)), dma((4, 4)),
             dma((7,)), dma((7,)), dma((7,)), dma((7,)),
             dma((4,)), dma((4,)), dma((4,)), dma((4,)), dma((4, 4)), dma((4, 4)),
             dma((4, 7)), dma((4, 7)), dma((1,)), dma((1,)),
+            dma((16,)), dma((1,)), dma((2, 2)), dma((2, 2)), dma((2, 2)), dma((2, 2)),
+            dma((2, 3)), dma((2, 3)), dma((2, 8)), dma((1,)),
         ],
         compiler_params=pltpu.CompilerParams(
             collective_id=0, has_side_effects=True, vmem_limit_bytes=60 * 1024 * 1024

time: 122 us -> 110 us (0.902)
  Pallas kernels: 120 us -> 108 us
    pallas_call x1, Pallas kernels: 120 us -> 108 us  [local(): pl.pallas_call(kernel, out_shape=jax.ShapeDtypeStruct((Q, TOK, PIECE), BF...]
where the time goes in v4:
time: 110 us; the launch traced here: 109 us
  Pallas kernels  108 us (98%)
  local copies, waits for them, and re-layouts  1.48 us (1%)
    pallas_call x1, Pallas kernels, local(): pl.pallas_call(kernel, out_shape=jax.ShapeDtypeStruct((Q, TOK, PIECE), BF...  108 us

profile of v4, /device:TPU:1, one launch (start us, length us, event | category | flops | bytes accessed | tf_op | source)
XLA Modules:
  0.0 109.3 jit_solution(10686959997800384639)
XLA Ops:
  0.0 107.8 %shard_map.64 = bf16[4,16,224]{2,1,0:T(8,128)(2,1)} custom-call(bf16[16,7168]{1,0:T(8,128)(2,1)} %tok_in.1, s32[8,16]{1,0:T(8,128)} %bitcast.10, f32[8,16]{1,0:T(8,128)} %bitcast.11, bf16[1792,256]{1,0:T(8,128)(2,1)} %bitcast.7, bf16[1792,256]{1,0:T(8,128)(2,1)} %bitcast.8, bf16[256,1792]{1,0:T(8,128)(2,1)} %bitcast.9), custom_call_target="tpu_custom_call" | custom-call | flops 3000000000 | bytes 4000000 | tf_op jit(solution)/shard_map/pallas_call | solution.py:497
  107.8 0.8 copy.7
  108.6 0.7 reshape.3

commit v5 on v4

--- a/solution.py
+++ b/solution.py
@@ -28,10 +28,10 @@
 def kernel(
     tok_in, routes_in, rw_in, gate_in, up_in, down_in, out,
     tok, routes, rw, xb, bb, wg, wu, wd, dj, acc, pbuf, pcore, ybuf, py, hid,
-    fmat, wbuf, rsend, rrecv, fin, ret, tx1, rx1, tx2, rx2, ty, ry, tz, rz,
+    fmat, wbuf, zs, zr, fin, ret, tx1, rx1, tx2, rx2, ty, ry, tz, rz,
     w_sem, g_send, g_recv, b_send, b_recv, x_send, x_recv, y_send, y_recv, bx_send, bx_recv,
     up_send, up_recv, dn_send, dn_recv,
-    p_send, p_recv, m_send, m_recv, h_send, h_recv, rs_send, rs_recv, a_send, a_recv,
+    p_send, p_recv, m_send, m_recv, h_send, h_recv, z_send, z_recv, a_send, a_recv,
     f_send, f_recv, r1_send, r1_recv, r2_send, r2_recv, ry_send, ry_recv, rz_send, rz_recv,
 ):
     p = lax.axis_index("expert")
@@ -83,19 +83,7 @@
         return carry
 
     lax.fori_loop(Q, Z * Q, greet_z, 0)
-    for load in loads[:3]:
-        load.wait()
-
-    named, share = routes[...], rw[...]
-    lane = lax.broadcasted_iota(jnp.int32, (TOK, TOK), 1)
-    diagonal = lane == lax.broadcasted_iota(jnp.int32, (TOK, TOK), 0)
-    wide = lax.broadcasted_iota(jnp.int32, (TOK, 128), 1)
-    factors = jnp.zeros((TOK, 128), F32)
-    for x in range(EXPERTS):
-        row = jnp.sum(jnp.where(named == x, share, 0.0), axis=0, keepdims=True)
-        factor = jnp.sum(jnp.where(diagonal, row, 0.0), axis=1, keepdims=True)
-        factors = jnp.where(wide == x, factor, factors)
-    fmat[...] = factors
+    loads[0].wait()
     pl.semaphore_wait(barrier, EXPERTS * Q - 1 + (Z - 1) * Q)
 
     side = jnp.where(z % 2 == 1, 1, Q - 1)
@@ -177,23 +165,6 @@
     for i in range(1, Q):
         y_sends(i)
 
-    def share_factors(i, carry):
-        to = (e + i) % EXPERTS * Q + share_of_column
-
-        @pl.when(to != p)
-        def _():
-            remote(fmat, wbuf.at[q, ey], f_send.at[i], f_recv.at[0], to, z).start()
-
-        @pl.when(to == p)
-        def _():
-            pltpu.make_async_copy(fmat, wbuf.at[q, ey], f_recv.at[0]).start()
-
-        return carry
-
-    share_of_column = (ex % 2) * 2 + ex // 2
-    lax.fori_loop(0, EXPERTS, share_factors, 0)
-    for load in loads[3:]:
-        load.wait()
     y_arrived(0)
     x_sends(0)
     for d in range(1, LX):
@@ -275,6 +246,36 @@
     for k in (0, 1):
         ring_send(k, 1)
         ring_send(k, -1)
+    for load in loads[1:]:
+        load.wait()
+
+    named, share = routes[...], rw[...]
+    lane = lax.broadcasted_iota(jnp.int32, (TOK, TOK), 1)
+    diagonal = lane == lax.broadcasted_iota(jnp.int32, (TOK, TOK), 0)
+    wide = lax.broadcasted_iota(jnp.int32, (TOK, 128), 1)
+    factors = jnp.zeros((TOK, 128), F32)
+    for x in range(EXPERTS):
+        row = jnp.sum(jnp.where(named == x, share, 0.0), axis=0, keepdims=True)
+        factor = jnp.sum(jnp.where(diagonal, row, 0.0), axis=1, keepdims=True)
+        factors = jnp.where(wide == x, factor, factors)
+    fmat[...] = factors
+
+
+    def share_factors(i, carry):
+        to = (e + i) % EXPERTS * Q + share_of_column
+
+        @pl.when(to != p)
+        def _():
+            remote(fmat, wbuf.at[q, ey], f_send.at[i], f_recv.at[0], to, z).start()
+
+        @pl.when(to == p)
+        def _():
+            pltpu.make_async_copy(fmat, wbuf.at[q, ey], f_recv.at[0]).start()
+
+        return carry
+
+    share_of_column = (ex % 2) * 2 + ex // 2
+    lax.fori_loop(0, EXPERTS, share_factors, 0)
     add_block(z, True)
     for j in range(Z):
         dj[j] = wd[:, j * PIECE : (j + 1) * PIECE]
@@ -322,39 +323,44 @@
         for d in range(1, Q):
             arrived(hid.at[order[i], rows(share_row((q + Q - d) % Q), SHARE)], h_recv.at[i, d])
 
-    chunks = (0, 2, 1, 3)
-
-    def way_of(c):
-        return 1 if c < 2 else -1
-
-    def sum_copy(c, s):
+    def z_part(ref, g, w, s, part):
+        return ref.at[g, w, s, part * SUB : (part + 1) * SUB]
+
+    def z_copy(g, w, s, part):
         return remote(
-            rsend.at[c, s], rrecv.at[c, s], rs_send.at[c, s], rs_recv.at[c, s],
-            p, z_up if way_of(c) > 0 else z_dn,
+            z_part(zs, g, w, s, part), z_part(zr, g, w, s, part), z_send.at[g, w, s, part],
+            z_recv.at[g, w, s, part], p, z_dn if w else z_up,
         )
 
-    def term(c, j):
-        return jnp.dot(hid[c // 2, c % 2 * SUB : (c % 2 + 1) * SUB, :], dj[j], preferred_element_type=F32)
-
-    def sum_step(s):
-        for c in chunks:
-            j = (z - way_of(c) * (1 + s) + 2 * Z) % Z
-            value = term(c, j)
-            if s > 0:
-                arrived(rrecv.at[c, s - 1], rs_recv.at[c, s - 1])
-                value += rrecv[c, s - 1].astype(F32)
-            rsend[c, s] = value.astype(BF)
-            sum_copy(c, s).start()
-
-    def sum_last(c):
-        value = term(c, z)
-        arrived(rrecv.at[c, Z - 2], rs_recv.at[c, Z - 2])
-        fin[c] = (value + rrecv[c, Z - 2].astype(F32)).astype(BF)
+    def term(g, part, j):
+        return jnp.dot(hid[g, part * SUB : (part + 1) * SUB, :], dj[j], preferred_element_type=F32)
+
+    def z_step(g, s):
+        for turn in (0, 1):
+            for w in (0, 1):
+                part = turn if w == 0 else 1 - turn
+                if s == 0 and part != w:
+                    continue
+                j = (z + (4 - s) * (1 - 2 * w) + Z) % Z
+                value = term(g, part, j)
+                if s > 1 or (s == 1 and part == w):
+                    arrived(z_part(zr, g, w, s - 1, part), z_recv.at[g, w, s - 1, part])
+                    value += zr[g, w, s - 1, part * SUB : (part + 1) * SUB, :].astype(F32)
+                zs[g, w, s, part * SUB : (part + 1) * SUB, :] = value.astype(BF)
+                z_copy(g, w, s, part).start()
+
+    def z_last(g):
+        for part in (0, 1):
+            value = term(g, part, z)
+            for w in (0, 1):
+                arrived(z_part(zr, g, w, 3, part), z_recv.at[g, w, 3, part])
+                value += zr[g, w, 3, part * SUB : (part + 1) * SUB, :].astype(F32)
+            fin[g, part * SUB : (part + 1) * SUB, :] = value.astype(BF)
 
         def home(i, carry):
-            to_e = c % 2 * (EXPERTS // 2) + (e + i) % (EXPERTS // 2)
-            to = to_e * Q + c // 2
-            src = fin.at[c, rows((e + i) % (EXPERTS // 2) * TOK, TOK)]
+            to_e = (e + i) % EXPERTS
+            to = to_e * Q + g
+            src = fin.at[g, rows(to_e * TOK, TOK)]
 
             @pl.when(to != p)
             def _():
@@ -366,7 +372,7 @@
 
             return carry
 
-        lax.fori_loop(0, EXPERTS // 2, home, 0)
+        lax.fori_loop(0, EXPERTS, home, 0)
 
     half = column // 2
 
@@ -423,22 +429,23 @@
             def _(j=j):
                 pltpu.make_async_copy(tz.at[t, j], rz.at[q, z], rz_recv.at[0]).start()
 
-    sum_step(0)
+    z_step(0, 0)
+    z_step(1, 0)
     plane_far(0)
     plane_far(1)
-    sum_step(1)
+    z_step(0, 1)
+    z_step(1, 1)
     plane_near(0)
-    sum_step(2)
+    z_step(0, 2)
     plane_near(1)
-    sum_step(3)
-    sum_step(4)
+    z_step(1, 2)
     plane_y(0)
-    sum_step(5)
+    z_step(0, 3)
+    z_step(1, 3)
     plane_y(1)
-    sum_step(6)
+    z_last(0)
     plane_home(0)
-    for c in chunks:
-        sum_last(c)
+    z_last(1)
     plane_home(1)
 
     @pl.when(q < 2)
@@ -479,9 +486,12 @@
         return carry
 
     lax.fori_loop(0, EXPERTS, factors_sent, 0)
-    for c in range(Q):
-        for s in range(Z - 1):
-            sum_copy(c, s).wait_send()
+    for g in range(2):
+        for w in range(2):
+            for s in range(4):
+                for part in range(2):
+                    if s > 0 or part == w:
+                        z_copy(g, w, s, part).wait_send()
     for t in range(2):
         for j in range(Z):
 
@@ -517,9 +527,9 @@
             pltpu.VMEM((Q, ROWS, UNITS), BF),
             pltpu.VMEM((TOK, 128), F32),
             pltpu.VMEM((Q, LY, TOK, 128), F32),
-            pltpu.VMEM((Q, Z - 1, SUB, PIECE), BF),
-            pltpu.VMEM((Q, Z - 1, SUB, PIECE), BF),
-            pltpu.VMEM((Q, SUB, PIECE), BF),
+            pltpu.VMEM((2, 2, 4, ROWS, PIECE), BF),
+            pltpu.VMEM((2, 2, 4, ROWS, PIECE), BF),
+            pltpu.VMEM((2, ROWS, PIECE), BF),
             pltpu.VMEM((EXPERTS * Q, TOK, PIECE), BF),
             pltpu.VMEM((2, SHARE, W), BF),
             pltpu.VMEM((2, 2, SHARE // 2, W), BF),
@@ -533,7 +543,7 @@
             dma((4, 4)), dma((4, 4)), dma((4, 4)), dma((4, 4)),
             dma((7,)), dma((7,)), dma((7,)), dma((7,)),
             dma((4,)), dma((4,)), dma((4,)), dma((4,)), dma((4, 4)), dma((4, 4)),
-            dma((4, 7)), dma((4, 7)), dma((1,)), dma((1,)),
+            dma((2, 2, 4, 2)), dma((2, 2, 4, 2)), dma((1,)), dma((1,)),
             dma((16,)), dma((1,)), dma((2, 2)), dma((2, 2)), dma((2, 2)), dma((2, 2)),
             dma((2, 3)), dma((2, 3)), dma((2, 8)), dma((1,)),
         ],

time: 110 us -> 106 us (0.964)
  Pallas kernels: 108 us -> 105 us
    pallas_call x1, Pallas kernels: 108 us -> 105 us  [local(): pl.pallas_call(kernel, out_shape=jax.ShapeDtypeStruct((Q, TOK, PIECE), BF...]
where the time goes in v5:
time: 106 us
  Pallas kernels  105 us (99%)
  local copies, waits for them, and re-layouts  1.48 us (1%)
    pallas_call x1, Pallas kernels, local(): pl.pallas_call(kernel, out_shape=jax.ShapeDtypeStruct((Q, TOK, PIECE), BF...  105 us

profile of v5, /device:TPU:1, one launch (start us, length us, event | category | flops | bytes accessed | tf_op | source)
XLA Modules:
  0.0 106.2 jit_solution(11574263379962704204)
XLA Ops:
  0.0 104.7 %shard_map.64 = bf16[4,16,224]{2,1,0:T(8,128)(2,1)} custom-call(bf16[16,7168]{1,0:T(8,128)(2,1)} %tok_in.1, s32[8,16]{1,0:T(8,128)} %bitcast.10, f32[8,16]{1,0:T(8,128)} %bitcast.11, bf16[1792,256]{1,0:T(8,128)(2,1)} %bitcast.7, bf16[1792,256]{1,0:T(8,128)(2,1)} %bitcast.8, bf16[256,1792]{1,0:T(8,128)(2,1)} %bitcast.9), custom_call_target="tpu_custom_call" | custom-call | flops 3000000000 | bytes 4000000 | tf_op jit(solution)/shard_map/pallas_call | solution.py:507
  104.7 0.8 copy.7
  105.5 0.7 reshape.3

commit v6 on v5

--- a/solution.py
+++ b/solution.py
@@ -14,7 +14,7 @@
 TOK = 16
 D = 7168
 W = D // Q
-PART = 384
+PART = 512
 REST = W - 2 * PART
 PIECE = W // Z
 UNITS = 256
@@ -429,22 +429,22 @@
             def _(j=j):
                 pltpu.make_async_copy(tz.at[t, j], rz.at[q, z], rz_recv.at[0]).start()
 
+    plane_far(0)
+    plane_far(1)
     z_step(0, 0)
     z_step(1, 0)
-    plane_far(0)
-    plane_far(1)
+    plane_near(0)
     z_step(0, 1)
     z_step(1, 1)
-    plane_near(0)
+    plane_near(1)
     z_step(0, 2)
-    plane_near(1)
+    plane_y(0)
     z_step(1, 2)
-    plane_y(0)
     z_step(0, 3)
+    plane_y(1)
     z_step(1, 3)
-    plane_y(1)
+    plane_home(0)
     z_last(0)
-    plane_home(0)
     z_last(1)
     plane_home(1)
 

time: 106 us -> 103 us (0.972)
  Pallas kernels: 105 us -> 102 us
    pallas_call x1, Pallas kernels: 105 us -> 102 us  [local(): pl.pallas_call(kernel, out_shape=jax.ShapeDtypeStruct((Q, TOK, PIECE), BF...]
where the time goes in v6:
time: 103 us
  Pallas kernels  102 us (99%)
  local copies, waits for them, and re-layouts  1.48 us (1%)
    pallas_call x1, Pallas kernels, local(): pl.pallas_call(kernel, out_shape=jax.ShapeDtypeStruct((Q, TOK, PIECE), BF...  102 us

profile of v6, /device:TPU:1, one launch (start us, length us, event | category | flops | bytes accessed | tf_op | source)
XLA Modules:
  0.0 103.2 jit_solution(16346428393227815166)
XLA Ops:
  0.0 101.7 %shard_map.64 = bf16[4,16,224]{2,1,0:T(8,128)(2,1)} custom-call(bf16[16,7168]{1,0:T(8,128)(2,1)} %tok_in.1, s32[8,16]{1,0:T(8,128)} %bitcast.10, f32[8,16]{1,0:T(8,128)} %bitcast.11, bf16[1792,256]{1,0:T(8,128)(2,1)} %bitcast.7, bf16[1792,256]{1,0:T(8,128)(2,1)} %bitcast.8, bf16[256,1792]{1,0:T(8,128)(2,1)} %bitcast.9), custom_call_target="tpu_custom_call" | custom-call | flops 3000000000 | bytes 4000000 | tf_op jit(solution)/shard_map/pallas_call | solution.py:507
  101.7 0.8 copy.7
  102.5 0.7 reshape.3

commit v7 on v6

--- a/solution.py
+++ b/solution.py
@@ -314,9 +314,9 @@
     cross(2)
     ring_step(6)
     add_block((z + 4) % Z, False)
-    share_hidden(2)
     add_rest(3)
     share_partials(3)
+    share_hidden(2)
     cross(3)
     share_hidden(3)
     for i in range(Q):

time: 103 us -> 103 us (level)
  no operation moved by 1% of the time
where the time goes in v7:
time: 103 us
  Pallas kernels  101 us (98%)
  local copies, waits for them, and re-layouts  1.48 us (1%)
    pallas_call x1, Pallas kernels, local(): pl.pallas_call(kernel, out_shape=jax.ShapeDtypeStruct((Q, TOK, PIECE), BF...  101 us

profile of v7, /device:TPU:1, one launch (start us, length us, event | category | flops | bytes accessed | tf_op | source)
XLA Modules:
  0.0 102.9 jit_solution(10492298971866854518)
XLA Ops:
  0.0 101.4 %shard_map.64 = bf16[4,16,224]{2,1,0:T(8,128)(2,1)} custom-call(bf16[16,7168]{1,0:T(8,128)(2,1)} %tok_in.1, s32[8,16]{1,0:T(8,128)} %bitcast.10, f32[8,16]{1,0:T(8,128)} %bitcast.11, bf16[1792,256]{1,0:T(8,128)(2,1)} %bitcast.7, bf16[1792,256]{1,0:T(8,128)(2,1)} %bitcast.8, bf16[256,1792]{1,0:T(8,128)(2,1)} %bitcast.9), custom_call_target="tpu_custom_call" | custom-call | flops 3000000000 | bytes 4000000 | tf_op jit(solution)/shard_map/pallas_call | solution.py:507
  101.4 0.8 copy.7
  102.2 0.7 reshape.3
